TPU v7x, 32 devices: a whole 2x2x4 slice. The times are simulated.
32 devices in a mesh: chol: 8 (over z, y), walk: 4 (over x, core).
Axes of the slice: x: 2, y: 2, z: 4, core: 2. Of those that a mesh axis runs over, the one named last changes fastest.
Arguments:
- green: bfloat16 [32, 128, 512], P(('chol', 'walk')), may hold values from -2 to 2
- cholesky_rotated_vectors: bfloat16 [32, 128, 512], P('chol'), may hold values from -0.25 to 0.25
- walker_weight: float32 [32], P(('chol', 'walk')), may hold values from 0.04 to 0.16
Outputs:
- green_cot: float32 [32, 128, 512], P(('chol', 'walk'))
- chol_grad: float32 [32, 128, 512], P('chol', None, 'walk')
All inputs are finite; a program needn't handle non-finite values.
Results may differ from a plain program's by a relative error of at most 0.0029.
Values may be sent and summed in bfloat16 or wider, within the bound.
A program may use at most 64 MiB of HBM per device.

v0:
```python
import jax
import jax.numpy as jnp
from jax import lax
from jax.sharding import PartitionSpec as P


def shifted(block, axis, distance):
    devices = range(lax.axis_size(axis))
    route = [((i - distance) % len(devices), i) for i in devices]
    return lax.ppermute(block, axis, route)


def visit_walker(cholesky_rotated_vectors, walker_green_matrix, weight):
    swapped_pair = jnp.einsum(
        "dpu,fu->dfp",
        cholesky_rotated_vectors,
        walker_green_matrix,
        preferred_element_type=jnp.float32,
    ).astype(jnp.bfloat16)
    green_term = jnp.einsum(
        "vij,vim->jm", swapped_pair, cholesky_rotated_vectors, preferred_element_type=jnp.float32
    )
    chol_term = weight * jnp.einsum(
        "klq,qt->klt", swapped_pair, walker_green_matrix, preferred_element_type=jnp.float32
    )
    return (green_term, chol_term)


def pick_weight(weight_values, anchor):
    positions = lax.iota(jnp.int32, weight_values.shape[0])
    return jnp.sum(jnp.where(positions == anchor, weight_values, 0.0))


def shards(green, cholesky_rotated_vectors, walker_weight):
    cholesky_owner_count = lax.axis_size("chol")
    my_index = lax.axis_index("chol")
    weight_values = lax.all_gather(walker_weight, "chol", axis=0, tiled=True)
    moving = green[0]
    own_green, own_chol = visit_walker(cholesky_rotated_vectors, moving, walker_weight[0])
    right_hops = cholesky_owner_count // 2
    leftward_hop_count = cholesky_owner_count - 1 - right_hops

    def right_step(hop_index, walker_green_matrix, carried_along, chol_sum):
        walker_green_matrix = shifted(walker_green_matrix, "chol", 1)
        carried_along = shifted(carried_along, "chol", 1)
        anchor = (my_index - hop_index) % cholesky_owner_count
        green_term, chol_term = visit_walker(
            cholesky_rotated_vectors, walker_green_matrix, pick_weight(weight_values, anchor)
        )
        return (walker_green_matrix, carried_along + green_term, chol_sum + chol_term)

    def left_step(hop_index, walker_green_matrix, carried_along, chol_sum):
        walker_green_matrix = shifted(walker_green_matrix, "chol", -1)
        carried_along = shifted(carried_along, "chol", -1)
        anchor = (my_index + hop_index) % cholesky_owner_count
        green_term, chol_term = visit_walker(
            cholesky_rotated_vectors, walker_green_matrix, pick_weight(weight_values, anchor)
        )
        return (walker_green_matrix, carried_along + green_term, chol_sum + chol_term)

    def both_steps(hop_index, states):
        right_green, right_carried, left_green, left_carried, chol_sum = states
        right_green, right_carried, chol_sum = right_step(
            hop_index, right_green, right_carried, chol_sum
        )
        left_green, left_carried, chol_sum = left_step(
            hop_index, left_green, left_carried, chol_sum
        )
        return (right_green, right_carried, left_green, left_carried, chol_sum)

    start_state = (moving, own_green, moving, jnp.zeros_like(own_green), own_chol)
    states = lax.fori_loop(1, leftward_hop_count + 1, both_steps, start_state)
    right_green, right_carried, left_green, left_carried, chol_sum = states
    right_green, right_carried, chol_sum = right_step(
        right_hops, right_green, right_carried, chol_sum
    )
    back_right = shifted(right_carried, "chol", -right_hops)
    back_left = shifted(left_carried, "chol", leftward_hop_count)
    total = back_right + back_left
    green_cot = (-walker_weight[0] * total)[None]
    chol_grad = -lax.psum_scatter(chol_sum, "walk", scatter_dimension=2, tiled=True)
    return (green_cot, chol_grad)


def solution(mesh):
    in_specs = (P(("chol", "walk"), None, None), P("chol", None, None), P(("chol", "walk")))
    out_specs = (P(("chol", "walk"), None, None), P("chol", None, "walk"))
    return jax.shard_map(shards, mesh=mesh, in_specs=in_specs, out_specs=out_specs, check_vma=False)
```

profile of v0, /device:TPU:0, one launch (start us, length us, event | category | flops | bytes accessed | tf_op | source)
XLA Modules:
  0.0 137.4 jit_solution(10136494637218988091)
XLA Ops:
  8.2 1.3 fusion.14
  12.7 23.2 %all-reduce = f32[8]{0:T(128)S(1)} all-reduce(f32[8]{0:T(128)S(1)} %dynamic-update-slice), channel_id=1, replica_groups=mesh['chol'=8,'walk'=4] {'chol'}, use_global_device_ids=true, to_apply=%add | all-reduce | flops 8 | bytes 64
  35.9 56.0 %while.24 = (s32[]{:T(128)}, bf16[128,512]{1,0:T(8,128)(2,1)S(1)}, f32[128,512]{1,0:T(8,128)S(1)}, bf16[128,512]{1,0:T(8,128)(2,1)S(1)}, f32[128,512]{1,0:T(8,12...) while((s32[]{:T(128)}, bf16[128,512]{1,0:T(8,128)(2,1)S(1)}, ...), condition=%wide.region_3.4_spmd.clone, body=%wide.region_0.3_spmd.clone.sunk | while | flops 404029472 | bytes 12845649 | solution.py:72
  36.2 4.5 %collective-permute-start.2 = (bf16[128,512]{1,0:T(8,128)(2,1)S(1)}, bf16[128,512]{1,0:T(8,128)(2,1)S(1)}, u32[]{:S(2)}, u32[]{:S(2)}) collective-permute-start(bf16[128,512]{1,0:T(8,128)(2,1)S(1)} %get-tuple-element.355), channel_id=1, source_target_pairs={{4,0},{8,4},{12,8},{16,12},{20,16},{24,20},{28,24},{0,28},{5,1},{9... | collective-permute-start | bytes 393224 | tf_op jit(solution)/shard_map/while/body/eval_jaxpr/ppermute | solution.py:10
  40.7 2.0 %collective-permute-start.3 = (f32[128,512]{1,0:T(8,128)S(1)}, f32[128,512]{1,0:T(8,128)S(1)}, u32[]{:S(2)}, u32[]{:S(2)}) collective-permute-start(f32[128,512]{1,0:T(8,128)S(1)} %broadcast_select_fusion.2), channel_id=1, source_target_pairs={{4,0},{8,4},{12,8},{16,12},{20,16},{24,20},{28,24},{0,28},{5,1},{9... | collective-permute-start | bytes 786440 | tf_op jit(solution)/shard_map/while/body/eval_jaxpr/ppermute | solution.py:10
  43.4 1.4 %collective-permute-done = bf16[128,512]{1,0:T(8,128)(2,1)S(1)} collective-permute-done((bf16[128,512]{1,0:T(8,128)(2,1)S(1)}, bf16[128,512]{1,0:T(8,128)(2,1)S(1)}, u32[]{:S(2)}, u32[]{:S(2)}) %collective-permute-start) | collective-permute-done | bytes 131104 | tf_op jit(solution)/shard_map/while/body/eval_jaxpr/ppermute | solution.py:10
  45.1 3.4 %collective-permute-done.2 = bf16[128,512]{1,0:T(8,128)(2,1)S(1)} collective-permute-done((bf16[128,512]{1,0:T(8,128)(2,1)S(1)}, bf16[128,512]{1,0:T(8,128)(2,1)S(1)}, u32[]{:S(2)}, u32[]{:S(2)}) %collective-permute-start.2) | collective-permute-done | bytes 131104 | tf_op jit(solution)/shard_map/while/body/eval_jaxpr/ppermute | solution.py:10
  49.7 1.1 fusion.72
  51.1 1.5 %collective-permute-done.3 = f32[128,512]{1,0:T(8,128)S(1)} collective-permute-done((f32[128,512]{1,0:T(8,128)S(1)}, f32[128,512]{1,0:T(8,128)S(1)}, u32[]{:S(2)}, u32[]{:S(2)}) %collective-permute-start.3) | collective-permute-done | bytes 262176 | tf_op jit(solution)/shard_map/while/body/eval_jaxpr/ppermute | solution.py:10
  53.0 4.7 %collective-permute-start.2 = (bf16[128,512]{1,0:T(8,128)(2,1)S(1)}, bf16[128,512]{1,0:T(8,128)(2,1)S(1)}, u32[]{:S(2)}, u32[]{:S(2)}) collective-permute-start(bf16[128,512]{1,0:T(8,128)(2,1)S(1)} %get-tuple-element.355), channel_id=1, source_target_pairs={{4,0},{8,4},{12,8},{16,12},{20,16},{24,20},{28,24},{0,28},{5,1},{9... | collective-permute-start | bytes 393224 | tf_op jit(solution)/shard_map/while/body/eval_jaxpr/ppermute | solution.py:10
  57.8 2.0 %collective-permute-start.3 = (f32[128,512]{1,0:T(8,128)S(1)}, f32[128,512]{1,0:T(8,128)S(1)}, u32[]{:S(2)}, u32[]{:S(2)}) collective-permute-start(f32[128,512]{1,0:T(8,128)S(1)} %broadcast_select_fusion.2), channel_id=1, source_target_pairs={{4,0},{8,4},{12,8},{16,12},{20,16},{24,20},{28,24},{0,28},{5,1},{9... | collective-permute-start | bytes 786440 | tf_op jit(solution)/shard_map/while/body/eval_jaxpr/ppermute | solution.py:10
  60.5 3.5 %collective-permute-done = bf16[128,512]{1,0:T(8,128)(2,1)S(1)} collective-permute-done((bf16[128,512]{1,0:T(8,128)(2,1)S(1)}, bf16[128,512]{1,0:T(8,128)(2,1)S(1)}, u32[]{:S(2)}, u32[]{:S(2)}) %collective-permute-start) | collective-permute-done | bytes 131104 | tf_op jit(solution)/shard_map/while/body/eval_jaxpr/ppermute | solution.py:10
  64.3 3.3 %collective-permute-done.2 = bf16[128,512]{1,0:T(8,128)(2,1)S(1)} collective-permute-done((bf16[128,512]{1,0:T(8,128)(2,1)S(1)}, bf16[128,512]{1,0:T(8,128)(2,1)S(1)}, u32[]{:S(2)}, u32[]{:S(2)}) %collective-permute-start.2) | collective-permute-done | bytes 131104 | tf_op jit(solution)/shard_map/while/body/eval_jaxpr/ppermute | solution.py:10
  70.2 1.9 %collective-permute-done.3 = f32[128,512]{1,0:T(8,128)S(1)} collective-permute-done((f32[128,512]{1,0:T(8,128)S(1)}, f32[128,512]{1,0:T(8,128)S(1)}, u32[]{:S(2)}, u32[]{:S(2)}) %collective-permute-start.3) | collective-permute-done | bytes 262176 | tf_op jit(solution)/shard_map/while/body/eval_jaxpr/ppermute | solution.py:10
  72.5 4.7 %collective-permute-start.2 = (bf16[128,512]{1,0:T(8,128)(2,1)S(1)}, bf16[128,512]{1,0:T(8,128)(2,1)S(1)}, u32[]{:S(2)}, u32[]{:S(2)}) collective-permute-start(bf16[128,512]{1,0:T(8,128)(2,1)S(1)} %get-tuple-element.355), channel_id=1, source_target_pairs={{4,0},{8,4},{12,8},{16,12},{20,16},{24,20},{28,24},{0,28},{5,1},{9... | collective-permute-start | bytes 393224 | tf_op jit(solution)/shard_map/while/body/eval_jaxpr/ppermute | solution.py:10
  77.2 2.0 %collective-permute-start.3 = (f32[128,512]{1,0:T(8,128)S(1)}, f32[128,512]{1,0:T(8,128)S(1)}, u32[]{:S(2)}, u32[]{:S(2)}) collective-permute-start(f32[128,512]{1,0:T(8,128)S(1)} %broadcast_select_fusion.2), channel_id=1, source_target_pairs={{4,0},{8,4},{12,8},{16,12},{20,16},{24,20},{28,24},{0,28},{5,1},{9... | collective-permute-start | bytes 786440 | tf_op jit(solution)/shard_map/while/body/eval_jaxpr/ppermute | solution.py:10
  79.9 3.9 %collective-permute-done = bf16[128,512]{1,0:T(8,128)(2,1)S(1)} collective-permute-done((bf16[128,512]{1,0:T(8,128)(2,1)S(1)}, bf16[128,512]{1,0:T(8,128)(2,1)S(1)}, u32[]{:S(2)}, u32[]{:S(2)}) %collective-permute-start) | collective-permute-done | bytes 131104 | tf_op jit(solution)/shard_map/while/body/eval_jaxpr/ppermute | solution.py:10
  84.1 2.5 %collective-permute-done.2 = bf16[128,512]{1,0:T(8,128)(2,1)S(1)} collective-permute-done((bf16[128,512]{1,0:T(8,128)(2,1)S(1)}, bf16[128,512]{1,0:T(8,128)(2,1)S(1)}, u32[]{:S(2)}, u32[]{:S(2)}) %collective-permute-start.2) | collective-permute-done | bytes 131104 | tf_op jit(solution)/shard_map/while/body/eval_jaxpr/ppermute | solution.py:10
  89.2 2.4 %collective-permute-done.3 = f32[128,512]{1,0:T(8,128)S(1)} collective-permute-done((f32[128,512]{1,0:T(8,128)S(1)}, f32[128,512]{1,0:T(8,128)S(1)}, u32[]{:S(2)}, u32[]{:S(2)}) %collective-permute-start.3) | collective-permute-done | bytes 262176 | tf_op jit(solution)/shard_map/while/body/eval_jaxpr/ppermute | solution.py:10
  92.5 7.0 %collective-permute-done.5 = bf16[128,512]{1,0:T(8,128)(2,1)S(1)} collective-permute-done((bf16[128,512]{1,0:T(8,128)(2,1)S(1)}, bf16[128,512]{1,0:T(8,128)(2,1)S(1)}, u32[]{:S(2)}, u32[]{:S(2)}) %collective-permute-start.5) | collective-permute-done | bytes 131104 | tf_op jit(solution)/shard_map/ppermute | solution.py:10
  99.9 1.9 %fusion.12 = f32[4,128,512]{2,1,0:T(8,128)} fusion(f32[4,128,512]{2,1,0:T(8,128)S(1)} %get-tuple-element.229, bf16[4,128,128]{2,1,0:T(8,128)(2,1)S(1)} %fusion.15, f32[]{:T(128)} %fusion.20, bf16[128,512]{1,0:T(8,128)(2,1)S(1)} %collective-permute-done.5), kind=kOutput, calls=%fused_computation.23 | convolution fusion | flops 67633152 | bytes 2359300 | tf_op jit(solution)/shard_map/klq,qt->klt/dot_general | solution.py:23
  102.0 11.9 %collective-permute-done.4 = f32[128,512]{1,0:T(8,128)S(1)} collective-permute-done((f32[128,512]{1,0:T(8,128)S(1)}, f32[128,512]{1,0:T(8,128)S(1)}, u32[]{:S(2)}, u32[]{:S(2)}) %collective-permute-start.4) | collective-permute-done | bytes 262176 | tf_op jit(solution)/shard_map/ppermute | solution.py:10
  115.0 13.1 %collective-permute-done.7 = f32[128,512]{1,0:T(8,128)S(1)} collective-permute-done((f32[128,512]{1,0:T(8,128)S(1)}, f32[128,512]{1,0:T(8,128)S(1)}, u32[]{:S(2)}, u32[]{:S(2)}) %collective-permute-start.7) | collective-permute-done | bytes 262176 | tf_op jit(solution)/shard_map/ppermute | solution.py:10
  128.9 1.7 %neg.7 = f32[4,128,128]{2,1,0:T(8,128)} negate(f32[4,128,128]{2,1,0:T(8,128)} %reduce-scatter.2.cloned.1.call-done) | non-fusion elementwise | flops 65536 | bytes 524288 | tf_op jit(solution)/shard_map/neg | solution.py:81
  (62 shorter events, 17.2 us)
Async XLA Ops:
  7.2 2.4 %copy-start = (bf16[4,128,512]{2,1,0:T(8,128)(2,1)S(1)}, bf16[4,128,512]{2,1,0:T(8,128)(2,1)}, u32[]{:S(2)}) copy-start(bf16[4,128,512]{2,1,0:T(8,128)(2,1)} %param.6) | copy-start | bytes 1572868
  7.2 121.7 %reduce-scatter.2.cloned.1.call-start = ((), (), s32[]{:S(2)}) async-start(), calls=%async_computation.1 | async-start | bytes 1310720 | tf_op jit(solution)/shard_map/reduce_scatter | solution.py:81
  10.8 0.7 copy-start.1
  35.9 8.9 %collective-permute-start = (bf16[128,512]{1,0:T(8,128)(2,1)S(1)}, bf16[128,512]{1,0:T(8,128)(2,1)S(1)}, u32[]{:S(2)}, u32[]{:S(2)}) collective-permute-start(bf16[128,512]{1,0:T(8,128)(2,1)S(1)} %get-tuple-element.353), channel_id=1, source_target_pairs={{28,0},{0,4},{4,8},{8,12},{12,16},{16,20},{20,24},{24,28},{29,1},{... | collective-permute-start | bytes 393224 | tf_op jit(solution)/shard_map/while/body/eval_jaxpr/ppermute | solution.py:10
  35.9 14.9 %collective-permute-start.1 = (f32[128,512]{1,0:T(8,128)S(1)}, f32[128,512]{1,0:T(8,128)S(1)}, u32[]{:S(2)}, u32[]{:S(2)}) collective-permute-start(f32[128,512]{1,0:T(8,128)S(1)} %get-tuple-element.354), channel_id=1, source_target_pairs={{28,0},{0,4},{4,8},{8,12},{12,16},{16,20},{20,24},{24,28},{29,1},{... | collective-permute-start | bytes 786440 | tf_op jit(solution)/shard_map/while/body/eval_jaxpr/ppermute | solution.py:10
  36.2 12.3 %collective-permute-start.2 = (bf16[128,512]{1,0:T(8,128)(2,1)S(1)}, bf16[128,512]{1,0:T(8,128)(2,1)S(1)}, u32[]{:S(2)}, u32[]{:S(2)}) collective-permute-start(bf16[128,512]{1,0:T(8,128)(2,1)S(1)} %get-tuple-element.355), channel_id=1, source_target_pairs={{4,0},{8,4},{12,8},{16,12},{20,16},{24,20},{28,24},{0,28},{5,1},{9... | collective-permute-start | bytes 393224 | tf_op jit(solution)/shard_map/while/body/eval_jaxpr/ppermute | solution.py:10
  40.7 11.9 %collective-permute-start.3 = (f32[128,512]{1,0:T(8,128)S(1)}, f32[128,512]{1,0:T(8,128)S(1)}, u32[]{:S(2)}, u32[]{:S(2)}) collective-permute-start(f32[128,512]{1,0:T(8,128)S(1)} %broadcast_select_fusion.2), channel_id=1, source_target_pairs={{4,0},{8,4},{12,8},{16,12},{20,16},{24,20},{28,24},{0,28},{5,1},{9... | collective-permute-start | bytes 786440 | tf_op jit(solution)/shard_map/while/body/eval_jaxpr/ppermute | solution.py:10
  52.9 11.0 %collective-permute-start = (bf16[128,512]{1,0:T(8,128)(2,1)S(1)}, bf16[128,512]{1,0:T(8,128)(2,1)S(1)}, u32[]{:S(2)}, u32[]{:S(2)}) collective-permute-start(bf16[128,512]{1,0:T(8,128)(2,1)S(1)} %get-tuple-element.353), channel_id=1, source_target_pairs={{28,0},{0,4},{4,8},{8,12},{12,16},{16,20},{20,24},{24,28},{29,1},{... | collective-permute-start | bytes 393224 | tf_op jit(solution)/shard_map/while/body/eval_jaxpr/ppermute | solution.py:10
  53.0 16.9 %collective-permute-start.1 = (f32[128,512]{1,0:T(8,128)S(1)}, f32[128,512]{1,0:T(8,128)S(1)}, u32[]{:S(2)}, u32[]{:S(2)}) collective-permute-start(f32[128,512]{1,0:T(8,128)S(1)} %get-tuple-element.354), channel_id=1, source_target_pairs={{28,0},{0,4},{4,8},{8,12},{12,16},{16,20},{20,24},{24,28},{29,1},{... | collective-permute-start | bytes 786440 | tf_op jit(solution)/shard_map/while/body/eval_jaxpr/ppermute | solution.py:10
  53.0 14.5 %collective-permute-start.2 = (bf16[128,512]{1,0:T(8,128)(2,1)S(1)}, bf16[128,512]{1,0:T(8,128)(2,1)S(1)}, u32[]{:S(2)}, u32[]{:S(2)}) collective-permute-start(bf16[128,512]{1,0:T(8,128)(2,1)S(1)} %get-tuple-element.355), channel_id=1, source_target_pairs={{4,0},{8,4},{12,8},{16,12},{20,16},{24,20},{28,24},{0,28},{5,1},{9... | collective-permute-start | bytes 393224 | tf_op jit(solution)/shard_map/while/body/eval_jaxpr/ppermute | solution.py:10
  57.8 14.3 %collective-permute-start.3 = (f32[128,512]{1,0:T(8,128)S(1)}, f32[128,512]{1,0:T(8,128)S(1)}, u32[]{:S(2)}, u32[]{:S(2)}) collective-permute-start(f32[128,512]{1,0:T(8,128)S(1)} %broadcast_select_fusion.2), channel_id=1, source_target_pairs={{4,0},{8,4},{12,8},{16,12},{20,16},{24,20},{28,24},{0,28},{5,1},{9... | collective-permute-start | bytes 786440 | tf_op jit(solution)/shard_map/while/body/eval_jaxpr/ppermute | solution.py:10
  72.4 11.4 %collective-permute-start = (bf16[128,512]{1,0:T(8,128)(2,1)S(1)}, bf16[128,512]{1,0:T(8,128)(2,1)S(1)}, u32[]{:S(2)}, u32[]{:S(2)}) collective-permute-start(bf16[128,512]{1,0:T(8,128)(2,1)S(1)} %get-tuple-element.353), channel_id=1, source_target_pairs={{28,0},{0,4},{4,8},{8,12},{12,16},{16,20},{20,24},{24,28},{29,1},{... | collective-permute-start | bytes 393224 | tf_op jit(solution)/shard_map/while/body/eval_jaxpr/ppermute | solution.py:10
  72.4 16.5 %collective-permute-start.1 = (f32[128,512]{1,0:T(8,128)S(1)}, f32[128,512]{1,0:T(8,128)S(1)}, u32[]{:S(2)}, u32[]{:S(2)}) collective-permute-start(f32[128,512]{1,0:T(8,128)S(1)} %get-tuple-element.354), channel_id=1, source_target_pairs={{28,0},{0,4},{4,8},{8,12},{12,16},{16,20},{20,24},{24,28},{29,1},{... | collective-permute-start | bytes 786440 | tf_op jit(solution)/shard_map/while/body/eval_jaxpr/ppermute | solution.py:10
  72.5 14.1 %collective-permute-start.2 = (bf16[128,512]{1,0:T(8,128)(2,1)S(1)}, bf16[128,512]{1,0:T(8,128)(2,1)S(1)}, u32[]{:S(2)}, u32[]{:S(2)}) collective-permute-start(bf16[128,512]{1,0:T(8,128)(2,1)S(1)} %get-tuple-element.355), channel_id=1, source_target_pairs={{4,0},{8,4},{12,8},{16,12},{20,16},{24,20},{28,24},{0,28},{5,1},{9... | collective-permute-start | bytes 393224 | tf_op jit(solution)/shard_map/while/body/eval_jaxpr/ppermute | solution.py:10
  77.2 14.3 %collective-permute-start.3 = (f32[128,512]{1,0:T(8,128)S(1)}, f32[128,512]{1,0:T(8,128)S(1)}, u32[]{:S(2)}, u32[]{:S(2)}) collective-permute-start(f32[128,512]{1,0:T(8,128)S(1)} %broadcast_select_fusion.2), channel_id=1, source_target_pairs={{4,0},{8,4},{12,8},{16,12},{20,16},{24,20},{28,24},{0,28},{5,1},{9... | collective-permute-start | bytes 786440 | tf_op jit(solution)/shard_map/while/body/eval_jaxpr/ppermute | solution.py:10
  91.8 7.7 %collective-permute-start.5 = (bf16[128,512]{1,0:T(8,128)(2,1)S(1)}, bf16[128,512]{1,0:T(8,128)(2,1)S(1)}, u32[]{:S(2)}, u32[]{:S(2)}) collective-permute-start(bf16[128,512]{1,0:T(8,128)(2,1)S(1)} %get-tuple-element.227), channel_id=1, source_target_pairs={{28,0},{0,4},{4,8},{8,12},{12,16},{16,20},{20,24},{24,28},{29,1},{... | collective-permute-start | bytes 393224 | tf_op jit(solution)/shard_map/ppermute | solution.py:10
  101.8 12.0 %collective-permute-start.4 = (f32[128,512]{1,0:T(8,128)S(1)}, f32[128,512]{1,0:T(8,128)S(1)}, u32[]{:S(2)}, u32[]{:S(2)}) collective-permute-start(f32[128,512]{1,0:T(8,128)S(1)} %get-tuple-element.226), channel_id=1, source_target_pairs={{28,0},{0,4},{4,8},{8,12},{12,16},{16,20},{20,24},{24,28},{29,1},{... | collective-permute-start | bytes 786440 | tf_op jit(solution)/shard_map/ppermute | solution.py:10
  101.9 26.2 %collective-permute-start.7 = (f32[128,512]{1,0:T(8,128)S(1)}, f32[128,512]{1,0:T(8,128)S(1)}, u32[]{:S(2)}, u32[]{:S(2)}) collective-permute-start(f32[128,512]{1,0:T(8,128)S(1)} %get-tuple-element.228), channel_id=1, source_target_pairs={{20,0},{24,4},{28,8},{0,12},{4,16},{8,20},{12,24},{16,28},{21,1},{... | collective-permute-start | bytes 786440 | tf_op jit(solution)/shard_map/ppermute | solution.py:10
  114.1 14.0 %collective-permute-start.6 = (f32[128,512]{1,0:T(8,128)S(1)}, f32[128,512]{1,0:T(8,128)S(1)}, u32[]{:S(2)}, u32[]{:S(2)}) collective-permute-start(f32[128,512]{1,0:T(8,128)S(1)} %fusion.13), channel_id=1, source_target_pairs={{16,0},{20,4},{24,8},{28,12},{0,16},{4,20},{8,24},{12,28},{17,1},{... | collective-permute-start | bytes 786440 | tf_op jit(solution)/shard_map/ppermute | solution.py:10
Sparse Core Ops, SparseCore 0:
  101.9 22.1 reduce-scatter.1
where the time goes:
time: 140 us; the launch traced here: 137 us
  waiting for transfers between devices  55.9 us (40%)
  blocking collectives  23.2 us (17%)
  starting transfers between devices  21.6 us (15%)
  between operations  14.8 us (11%)
  matrix products  13.6 us (10%)
  other arithmetic  5.07 us (4%)
  local copies, waits for them, and re-layouts  2.93 us (2%)
    ppermute x16, waiting for transfers between devices, shifted(): return lax.ppermute(block, axis, route)  55.9 us
    unnamed x1, blocking collectives  23.2 us
    ppermute x16, starting transfers between devices, shifted(): return lax.ppermute(block, axis, route)  21.6 us
    dot_general x8, matrix products, visit_walker(): jnp.einsum('klq,qt->klt', swapped_pair, walker_green_matrix, preferred_el...  8.1 us
    dot_general x8, matrix products, visit_walker(): jnp.einsum('dpu,fu->dfp', cholesky_rotated_vectors, walker_green_matrix,...  3.47 us
    unnamed x9, local copies, waits for them, and re-layouts  2.87 us
  transfers between devices with their start and end apart: 17, of which 12 were waited for; matrix products, arithmetic and copies ran while one was open for 9% of the time, Pallas kernels for 0%

commit v1 on v0

v1 whole, which is shorter than its diff:
```python
import functools

import jax
import jax.numpy as jnp
from jax import lax
from jax.experimental import pallas as pl
from jax.experimental.pallas import tpu as pltpu
from jax.sharding import PartitionSpec as P

MESH = pl.DeviceIdType.MESH
F32 = jnp.float32
BF16 = jnp.bfloat16
NT = (((1,), (1,)), ((), ()))
TN = (((0,), (0,)), ((), ()))


def each(count, body):
    if count <= 8:
        for step in range(count):
            body(step)
    else:
        lax.fori_loop(0, count, lambda step, _: (body(step), 0)[1], 0)


def kernel(
    depth, walk, weight_ref, green_ref, chol_ref, cot_ref, grad_ref,
    weight_tile, weights, greens, other, total, own_cot, cot_out, cot_in, grad_out, grad_in,
    green_sem, weight_sem, half_sem, mate_sem, cot_sem, grad_sem,
):
    me_c, me_k = lax.axis_index("chol"), lax.axis_index("walk")
    z, y = me_c // 2, me_c % 2
    pair = z * 2 + (1 - y)
    core = me_k % 2
    mate = me_k + 1 - 2 * core
    vectors, occupied, orbitals = chol_ref.shape
    half = vectors // 2
    rows = vectors * occupied
    part = orbitals // walk

    def up(step):
        return (((z + step) % depth) * 2 + y, me_k)

    def down(step):
        return (((z + depth - step) % depth) * 2 + y, me_k)

    def plane(index):
        return (z * 2 + (y + index // walk) % 2, (me_k + index % walk) % walk)

    barrier = pltpu.get_barrier_semaphore()

    def greet(device):
        pl.semaphore_signal(barrier, inc=1, device_id=device, device_id_type=MESH)

    each(depth - 1, lambda s: greet(up(s + 1)))
    for index in range(1, 2 * walk):
        greet(plane(index))
    pl.semaphore_wait(barrier, depth - 1 + 2 * walk - 1)

    def remote(src, dst, sems, index, device):
        return pltpu.make_async_remote_copy(
            src_ref=src, dst_ref=dst, send_sem=sems.at[0, index], recv_sem=sems.at[1, index],
            device_id=device, device_id_type=MESH,
        )

    def send_green(s):
        return remote(green_ref.at[0], greens.at[s], green_sem, s, up(s + 1))

    def send_weight(s):
        return remote(weight_tile, weights.at[s], weight_sem, s, up(s + 1))

    def send_cot(s):
        return remote(cot_out.at[s], cot_in.at[s], cot_sem, s, down(s + 1))

    def send_grad(index):
        return remote(
            grad_out.at[index - 1], grad_in.at[index - 1], grad_sem, index - 1, plane(index)
        )

    mine = pl.ds(core * half, half)
    send_half = remote(chol_ref.at[mine], other.at[mine], half_sem, 0, (pair, me_k))
    send_mate = remote(other.at[mine], other.at[mine], mate_sem, 0, (me_c, mate))

    send_half.start()
    each(depth - 1, lambda s: send_green(s).start())
    weight = weight_ref[0]
    weight_tile[...] = jnp.full(weight_tile.shape, weight, F32)
    each(depth - 1, lambda s: send_weight(s).start())

    def visit(walker, scale, vectors_ref, base, first):
        block = vectors_ref[...].reshape(rows, orbitals)
        swapped = lax.dot_general(block, walker, NT, preferred_element_type=F32).astype(BF16)
        pieces = [swapped[v * occupied:(v + 1) * occupied] for v in range(vectors)]
        cot = jnp.dot(jnp.concatenate(pieces, axis=1), block, preferred_element_type=F32)
        for v in range(vectors):
            term = scale * lax.dot_general(pieces[v], walker, TN, preferred_element_type=F32)
            at = pl.ds(base * rows + v * occupied, occupied)
            if first:
                total[at, :] = term
            else:
                total[at, :] += term
        return cot

    own_cot[...] = visit(green_ref[0], weight, chol_ref, 0, True)
    send_half.wait_recv()
    send_mate.start()
    send_mate.wait_recv()
    own_cot[...] += visit(green_ref[0], weight, other, 1, True)

    def visitor(s):
        send_green(s).wait_recv()
        send_weight(s).wait_recv()
        walker = greens[s]
        scale = weights[s][0:1, 0:1]
        cot = visit(walker, scale, chol_ref, 0, False) + visit(walker, scale, other, 1, False)
        cot_out[s] = cot.astype(BF16)
        send_cot(s).start()

    each(depth - 1, visitor)

    for index in range(1, 2 * walk):
        column = pl.multiple_of(((me_k + index % walk) % walk) * part, part)
        at = pl.ds((index // walk) * rows, rows)
        grad_out[index - 1] = total[at, pl.ds(column, part)].astype(BF16)
        send_grad(index).start()

    def add_cot(s):
        send_cot(s).wait_recv()
        own_cot[...] += cot_in[s].astype(F32)

    each(depth - 1, add_cot)
    cot_ref[0] = -weight * own_cot[...]
    grad = total[pl.ds(0, rows), pl.ds(pl.multiple_of(me_k * part, part), part)]
    for index in range(1, 2 * walk):
        send_grad(index).wait_recv()
        grad += grad_in[index - 1].astype(F32)
    grad_ref[...] = -grad.reshape(vectors, occupied, part)

    send_half.wait_send()
    send_mate.wait_send()
    for index in range(1, 2 * walk):
        send_grad(index).wait_send()

    def finish(s):
        send_green(s).wait_send()
        send_weight(s).wait_send()
        send_cot(s).wait_send()

    each(depth - 1, finish)


def shards(green, chol, weight):
    depth = lax.axis_size("chol") // 2
    walk = lax.axis_size("walk")
    vectors, occupied, orbitals = chol.shape
    rows = vectors * occupied
    part = orbitals // walk
    others = depth - 1
    vmem = pl.BlockSpec(memory_space=pltpu.VMEM)
    dma = pltpu.SemaphoreType.DMA
    return pl.pallas_call(
        functools.partial(kernel, depth, walk),
        out_shape=(
            jax.ShapeDtypeStruct((1, occupied, orbitals), F32),
            jax.ShapeDtypeStruct((vectors, occupied, part), F32),
        ),
        in_specs=[pl.BlockSpec(memory_space=pltpu.SMEM), vmem, vmem],
        out_specs=(vmem, vmem),
        scratch_shapes=[
            pltpu.VMEM((8, 128), F32),
            pltpu.VMEM((others, 8, 128), F32),
            pltpu.VMEM((others, occupied, orbitals), BF16),
            pltpu.VMEM((vectors, occupied, orbitals), BF16),
            pltpu.VMEM((2 * rows, orbitals), F32),
            pltpu.VMEM((occupied, orbitals), F32),
            pltpu.VMEM((others, occupied, orbitals), BF16),
            pltpu.VMEM((others, occupied, orbitals), BF16),
            pltpu.VMEM((2 * walk - 1, rows, part), BF16),
            pltpu.VMEM((2 * walk - 1, rows, part), BF16),
            dma((2, others)), dma((2, others)), dma((2, 1)), dma((2, 1)),
            dma((2, others)), dma((2, 2 * walk - 1)),
        ],
        compiler_params=pltpu.CompilerParams(
            collective_id=0, has_side_effects=True, vmem_limit_bytes=48 * 1024 * 1024
        ),
    )(weight, green, chol)


def solution(mesh):
    in_specs = (P(("chol", "walk"), None, None), P("chol", None, None), P(("chol", "walk")))
    out_specs = (P(("chol", "walk"), None, None), P("chol", None, "walk"))
    return jax.shard_map(shards, mesh=mesh, in_specs=in_specs, out_specs=out_specs, check_vma=False)
```

time: 140 us -> 38.7 us (0.28)
  the two profiles are of different devices: /device:TPU:0 before, /device:TPU:1 now
where the time goes in v1:
time: 38.7 us; the launch traced here: 38.5 us
  Pallas kernels  33.9 us (88%)
  local copies, waits for them, and re-layouts  3.35 us (9%)
  between operations  1.29 us (3%)
    pallas_call x1, Pallas kernels, shards(): pl.pallas_call(functools.partial(kernel, depth, walk), out_shape=(jax.Sha...  33.9 us
    unnamed x6, local copies, waits for them, and re-layouts  3.35 us

profile of v1, /device:TPU:1, one launch (start us, length us, event | category | flops | bytes accessed | tf_op | source)
XLA Modules:
  0.0 38.5 jit_solution(14355367587021722778)
XLA Ops:
  1.3 0.0 copy-start
  1.3 1.0 %copy-done = bf16[4,128,512]{2,1,0:T(8,128)(2,1)S(1)} copy-done((bf16[4,128,512]{2,1,0:T(8,128)(2,1)S(1)}, bf16[4,128,512]{2,1,0:T(8,128)(2,1)}, u32[]{:S(2)}) %copy-start) | copy-done | bytes 524312
  2.3 0.0 copy-start.1
  2.3 0.9 %copy-done.1 = bf16[1,128,512]{2,1,0:T(8,128)(2,1)S(1)} copy-done((bf16[1,128,512]{2,1,0:T(8,128)(2,1)S(1)}, bf16[1,128,512]{2,1,0:T(8,128)(2,1)}, u32[]{:S(2)}) %copy-start.1) | copy-done | bytes 131096
  3.2 33.9 %shard_map.50 = (f32[1,128,512]{2,1,0:T(8,128)S(1)}, f32[4,128,128]{2,1,0:T(8,128)S(1)}) custom-call(f32[1]{0:T(128)S(6)} %copy.7.weight_ref, bf16[1,128,512]{2,1,0:T(8,128)(2,1)S(1)} %copy-done.1, bf16[4,128,512]{2,1,0:T(8,128)(2,1)S(1)} %copy-done), custom_call_target="tpu_custom_call" | custom-call | tf_op jit(solution)/shard_map/pallas_call | solution.py:160
  37.1 0.7 %copy.8 = f32[1,128,512]{2,1,0:T(8,128)} copy(f32[1,128,512]{2,1,0:T(8,128)S(1)} %get-tuple-element.4) | data formatting | bytes 524288
  37.8 0.7 %copy.9 = f32[4,128,128]{2,1,0:T(8,128)} copy(f32[4,128,128]{2,1,0:T(8,128)S(1)} %get-tuple-element.5) | data formatting | bytes 524288
Async XLA Ops:
  1.3 1.0 %copy-start = (bf16[4,128,512]{2,1,0:T(8,128)(2,1)S(1)}, bf16[4,128,512]{2,1,0:T(8,128)(2,1)}, u32[]{:S(2)}) copy-start(bf16[4,128,512]{2,1,0:T(8,128)(2,1)} %chol_ref.1) | copy-start | bytes 1572868
  2.3 0.9 %copy-start.1 = (bf16[1,128,512]{2,1,0:T(8,128)(2,1)S(1)}, bf16[1,128,512]{2,1,0:T(8,128)(2,1)}, u32[]{:S(2)}) copy-start(bf16[1,128,512]{2,1,0:T(8,128)(2,1)} %green_ref.1) | copy-start | bytes 393220

commit v2 on v1

v2 whole, which is shorter than its diff:
```python
import functools

import jax
import jax.numpy as jnp
from jax import lax
from jax.experimental import pallas as pl
from jax.experimental.pallas import tpu as pltpu
from jax.sharding import PartitionSpec as P

MESH = pl.DeviceIdType.MESH
F32 = jnp.float32
BF16 = jnp.bfloat16
NT = (((1,), (1,)), ((), ()))
TN = (((0,), (0,)), ((), ()))


def each(count, body):
    if count <= 8:
        for step in range(count):
            body(step)
    else:
        lax.fori_loop(0, count, lambda step, _: (body(step), 0)[1], 0)


def kernel(
    deep, wide, weight_ref, green_hbm, chol_hbm, cot_ref, grad_ref,
    green, chol, other, weight_tile, weights, near_green, hi_green, far_green,
    total, own_cot, near_part, hi_part, near_out, near_in, far_out, far_in, hi_out, hi_in,
    mate_out, mate_in, grad_out, grad_in,
    load_sem, half_sem, share_sem, near_sem, hi_sem, far_sem, weight_sem,
    near_cot_sem, far_cot_sem, hi_cot_sem, mate_sem, grad_sem,
):
    me_c, me_k = lax.axis_index("chol"), lax.axis_index("walk")
    hi, lo, y = me_c // 4, (me_c // 2) % 2, me_c % 2
    x, core = me_k // 2, me_k % 2
    vectors, occupied, orbitals = chol.shape
    half = vectors // 2
    rows = vectors * occupied
    part = orbitals // (2 * wide)
    steps = deep - 1

    def on_line(distance, flip):
        position = ((hi + distance) % deep) * 2 + (lo + flip) % 2
        return (position * 2 + y, me_k)

    def on_plane(flip, distance):
        return ((hi * 2 + lo) * 2 + (y + flip) % 2, ((x + distance) % wide) * 2 + core)

    near = on_line(0, 1)
    pair = on_plane(1, 0)
    mate = (me_c, x * 2 + (1 - core))
    units = [(flip, j) for flip in (1, 0) for j in reversed(range(wide))]

    loads = [
        pltpu.make_async_copy(green_hbm.at[0], green, load_sem.at[0]),
        pltpu.make_async_copy(chol_hbm, chol, load_sem.at[1]),
    ]
    for load in loads:
        load.start()

    barrier = pltpu.get_barrier_semaphore()

    def greet(device):
        pl.semaphore_signal(barrier, inc=1, device_id=device, device_id_type=MESH)

    greet(near)
    greet(mate)

    def greet_line(s):
        greet(on_line(s + 1, 0))
        greet(on_line(s + 1, 1))

    each(steps, greet_line)
    for flip, j in units[:-1]:
        greet(on_plane(flip, j))
    pl.semaphore_wait(barrier, 2 + 2 * steps + len(units) - 1)

    def remote(src, dst, sems, index, device):
        return pltpu.make_async_remote_copy(
            src_ref=src, dst_ref=dst, send_sem=sems.at[0, index], recv_sem=sems.at[1, index],
            device_id=device, device_id_type=MESH,
        )

    mine = pl.ds(core * half, half)
    send_half = remote(chol.at[mine], other.at[mine], half_sem, 0, pair)
    send_share = remote(other.at[mine], other.at[mine], share_sem, 0, mate)
    send_near = remote(green, near_green, near_sem, 0, near)
    send_near_weight = remote(weight_tile, weights.at[0], weight_sem, 0, near)
    send_near_cot = remote(near_out, near_in, near_cot_sem, 0, near)

    def send_hi(s):
        return remote(green, hi_green.at[s], hi_sem, s, on_line(s + 1, 0))

    def send_far(s):
        return remote(hi_green.at[s], far_green.at[s], far_sem, s, near)

    def send_weight(s, flip):
        slot = 1 + 2 * s + flip
        return remote(weight_tile, weights.at[slot], weight_sem, slot, on_line(s + 1, flip))

    def send_far_cot(s):
        return remote(far_out.at[s], far_in.at[s], far_cot_sem, s, near)

    def send_hi_cot(s):
        return remote(hi_out.at[s], hi_in.at[s], hi_cot_sem, s, on_line(deep - 1 - s, 0))

    def send_mate(u):
        return remote(mate_out.at[u], mate_in.at[u], mate_sem, u, mate)

    def send_grad(u):
        return remote(grad_out.at[u], grad_in.at[u], grad_sem, u, on_plane(*units[u]))

    loads[0].wait()
    send_near.start()
    each(steps, lambda s: send_hi(s).start())
    loads[1].wait()
    send_half.start()
    weight = weight_ref[0]
    weight_tile[...] = jnp.full(weight_tile.shape, weight, F32)
    send_near_weight.start()

    def start_weights(s):
        send_weight(s, 0).start()
        send_weight(s, 1).start()

    each(steps, start_weights)

    def visit(walker, scale, vectors_ref, base, first):
        block = vectors_ref[...].reshape(rows, orbitals)
        swapped = lax.dot_general(block, walker, NT, preferred_element_type=F32).astype(BF16)
        pieces = [swapped[v * occupied:(v + 1) * occupied] for v in range(vectors)]
        cot = jnp.dot(jnp.concatenate(pieces, axis=1), block, preferred_element_type=F32)
        for v in range(vectors):
            term = scale * lax.dot_general(pieces[v], walker, TN, preferred_element_type=F32)
            at = pl.ds(base * rows + v * occupied, occupied)
            if first:
                total[at, :] = term
            else:
                total[at, :] += term
        return cot

    def scale_of(slot):
        return weights[slot][0:1, 0:1]

    own_cot[...] = visit(green[...], weight, chol, 0, True)
    send_near.wait_recv()
    send_near_weight.wait_recv()
    near_part[...] = visit(near_green[...], scale_of(0), chol, 0, False)
    send_half.wait_recv()
    send_share.start()

    def meet_hi(s):
        send_hi(s).wait_recv()
        send_far(s).start()
        send_weight(s, 0).wait_recv()
        hi_part[s] = visit(hi_green[s], scale_of(1 + 2 * s), chol, 0, False)

    each(steps, meet_hi)
    send_share.wait_recv()
    cot = near_part[...] + visit(near_green[...], scale_of(0), other, 1, True)
    near_out[...] = cot.astype(BF16)
    send_near_cot.start()
    own_cot[...] += visit(green[...], weight, other, 1, False)

    def finish_hi(s):
        hi_part[s] += visit(hi_green[s], scale_of(1 + 2 * s), other, 1, False)

    each(steps, finish_hi)

    def meet_far(s):
        send_far(s).wait_recv()
        send_weight(s, 1).wait_recv()
        scale = scale_of(2 + 2 * s)
        cot = visit(far_green[s], scale, chol, 0, False)
        cot += visit(far_green[s], scale, other, 1, False)
        far_out[s] = cot.astype(BF16)
        send_far_cot(s).start()

    each(steps, meet_far)

    def piece(unit, of_core):
        flip, j = unit
        column = pl.multiple_of((((x + j) % wide) * 2 + of_core) * part, part)
        return total[pl.ds(flip * rows, rows), pl.ds(column, part)]

    for u, unit in enumerate(units):
        mate_out[u] = piece(unit, 1 - core).astype(BF16)
        send_mate(u).start()
    for u, unit in enumerate(units[:-1]):
        send_mate(u).wait_recv()
        grad_out[u] = (piece(unit, core) + mate_in[u].astype(F32)).astype(BF16)
        send_grad(u).start()

    def pass_hi(s):
        send_far_cot(s).wait_recv()
        hi_out[s] = (hi_part[s] + far_in[s].astype(F32)).astype(BF16)
        send_hi_cot(s).start()

    each(steps, pass_hi)

    last = len(units) - 1
    send_mate(last).wait_recv()
    grad = piece(units[last], core) + mate_in[last].astype(F32)
    for u in range(last):
        send_grad(u).wait_recv()
        grad += grad_in[u].astype(F32)
    grad_ref[...] = -grad.reshape(vectors, occupied, part)

    send_near_cot.wait_recv()
    own_cot[...] += near_in[...].astype(F32)

    def add_hi(s):
        send_hi_cot(s).wait_recv()
        own_cot[...] += hi_in[s].astype(F32)

    each(steps, add_hi)
    cot_ref[0] = -weight * own_cot[...]

    for copy in (send_half, send_share, send_near, send_near_weight, send_near_cot):
        copy.wait_send()

    def finish(s):
        for copy in (
            send_hi(s), send_far(s), send_weight(s, 0), send_weight(s, 1),
            send_far_cot(s), send_hi_cot(s),
        ):
            copy.wait_send()

    each(steps, finish)
    for u in range(len(units)):
        send_mate(u).wait_send()
    for u in range(last):
        send_grad(u).wait_send()


def shards(green, chol, weight):
    deep = lax.axis_size("chol") // 4
    wide = lax.axis_size("walk") // 2
    vectors, occupied, orbitals = chol.shape
    rows = vectors * occupied
    part = orbitals // (2 * wide)
    steps = deep - 1
    units = 2 * wide
    matrix = (occupied, orbitals)
    vmem = pl.BlockSpec(memory_space=pltpu.VMEM)
    anywhere = pl.BlockSpec(memory_space=pl.ANY)
    dma = pltpu.SemaphoreType.DMA
    return pl.pallas_call(
        functools.partial(kernel, deep, wide),
        out_shape=(
            jax.ShapeDtypeStruct((1, occupied, orbitals), F32),
            jax.ShapeDtypeStruct((vectors, occupied, part), F32),
        ),
        in_specs=[pl.BlockSpec(memory_space=pltpu.SMEM), anywhere, anywhere],
        out_specs=(vmem, vmem),
        scratch_shapes=[
            pltpu.VMEM(matrix, BF16),
            pltpu.VMEM((vectors,) + matrix, BF16),
            pltpu.VMEM((vectors,) + matrix, BF16),
            pltpu.VMEM((8, 128), F32),
            pltpu.VMEM((1 + 2 * steps, 8, 128), F32),
            pltpu.VMEM(matrix, BF16),
            pltpu.VMEM((steps,) + matrix, BF16),
            pltpu.VMEM((steps,) + matrix, BF16),
            pltpu.VMEM((2 * rows, orbitals), F32),
            pltpu.VMEM(matrix, F32),
            pltpu.VMEM(matrix, F32),
            pltpu.VMEM((steps,) + matrix, F32),
            pltpu.VMEM(matrix, BF16),
            pltpu.VMEM(matrix, BF16),
            pltpu.VMEM((steps,) + matrix, BF16),
            pltpu.VMEM((steps,) + matrix, BF16),
            pltpu.VMEM((steps,) + matrix, BF16),
            pltpu.VMEM((steps,) + matrix, BF16),
            pltpu.VMEM((units, rows, part), BF16),
            pltpu.VMEM((units, rows, part), BF16),
            pltpu.VMEM((units - 1, rows, part), BF16),
            pltpu.VMEM((units - 1, rows, part), BF16),
            dma((2,)), dma((2, 1)), dma((2, 1)), dma((2, 1)), dma((2, steps)), dma((2, steps)),
            dma((2, 1 + 2 * steps)), dma((2, 1)), dma((2, steps)), dma((2, steps)),
            dma((2, units)), dma((2, units - 1)),
        ],
        compiler_params=pltpu.CompilerParams(
            collective_id=0, has_side_effects=True, vmem_limit_bytes=60 * 1024 * 1024
        ),
    )(weight, green, chol)


def solution(mesh):
    in_specs = (P(("chol", "walk"), None, None), P("chol", None, None), P(("chol", "walk")))
    out_specs = (P(("chol", "walk"), None, None), P("chol", None, "walk"))
    return jax.shard_map(shards, mesh=mesh, in_specs=in_specs, out_specs=out_specs, check_vma=False)
```

time: 38.7 us -> 35.7 us (0.922)
  the two profiles are of different devices: /device:TPU:1 before, /device:TPU:0 now
where the time goes in v2:
time: 35.7 us; the launch traced here: 35.5 us
  Pallas kernels  31.8 us (89%)
  local copies, waits for them, and re-layouts  2.42 us (7%)
  between operations  1.29 us (4%)
    pallas_call x1, Pallas kernels, shards(): pl.pallas_call(functools.partial(kernel, deep, wide), out_shape=(jax.Shap...  31.8 us
    unnamed x4, local copies, waits for them, and re-layouts  2.42 us

profile of v2, /device:TPU:0, one launch (start us, length us, event | category | flops | bytes accessed | tf_op | source)
XLA Modules:
  0.0 35.5 jit_solution(13037964187479286106)
XLA Ops:
  1.3 31.8 %shard_map.50 = (f32[1,128,512]{2,1,0:T(8,128)}, f32[4,128,128]{2,1,0:T(8,128)}) custom-call(f32[1]{0:T(128)S(6)} %copy.7.weight_ref, bf16[1,128,512]{2,1,0:T(8,128)(2,1)} %green_hbm.1, bf16[4,128,512]{2,1,0:T(8,128)(2,1)} %chol_hbm.1), custom_call_target="tpu_custom_call" | custom-call | tf_op jit(solution)/shard_map/pallas_call | solution.py:248
  33.1 0.0 copy-start
  33.1 1.7 %copy.8 = f32[1,128,512]{2,1,0:T(8,128)} copy(f32[1,128,512]{2,1,0:T(8,128)} %get-tuple-element.4) | data formatting | bytes 524288
  34.8 0.0 copy-done
  34.8 0.7 %copy.9 = f32[4,128,128]{2,1,0:T(8,128)} copy(f32[4,128,128]{2,1,0:T(8,128)S(1)} %copy-done) | data formatting | bytes 524288
Async XLA Ops:
  33.1 1.7 %copy-start = (f32[4,128,128]{2,1,0:T(8,128)S(1)}, f32[4,128,128]{2,1,0:T(8,128)}, u32[]{:S(2)}) copy-start(f32[4,128,128]{2,1,0:T(8,128)} %get-tuple-element.5) | copy-start | bytes 786436

commit v3 on v2

v3 whole, which is shorter than its diff:
```python
import functools

import jax
import jax.numpy as jnp
from jax import lax
from jax.experimental import pallas as pl
from jax.experimental.pallas import tpu as pltpu
from jax.sharding import PartitionSpec as P

MESH = pl.DeviceIdType.MESH
F32 = jnp.float32
BF16 = jnp.bfloat16
NT = (((1,), (1,)), ((), ()))
CHUNKS = 2
VMEM_BYTES = 60 * 1024 * 1024


def each(count, body):
    if count <= 8:
        for step in range(count):
            body(step)
    else:
        lax.fori_loop(0, count, lambda step, _: (body(step), 0)[1], 0)


def kernel(
    deep, wide, weight_ref, green_hbm, chol_hbm, cot_ref, grad_ref,
    walkers, block, weight_tile, weights, total, own_cot, hi_part,
    near_out, near_in, far_out, far_in, hi_out, hi_in,
    mate_out, mate_in, grad_out, grad_in,
    load_sem, half_sem, share_sem, near_sem, hi_sem, far_sem, weight_sem,
    near_cot_sem, far_cot_sem, hi_cot_sem, mate_sem, grad_sem,
):
    me_c, me_k = lax.axis_index("chol"), lax.axis_index("walk")
    hi, lo, y = me_c // 4, (me_c // 2) % 2, me_c % 2
    x, core = me_k // 2, me_k % 2
    occupied, orbitals = walkers.shape[1:]
    rows = block.shape[0] // 2
    vectors = rows // occupied
    half = rows // 2
    part = orbitals // (2 * wide)
    steps = deep - 1
    cut = occupied // CHUNKS

    def on_line(distance, flip):
        position = ((hi + distance) % deep) * 2 + (lo + flip) % 2
        return (position * 2 + y, me_k)

    def on_plane(flip, distance):
        return ((hi * 2 + lo) * 2 + (y + flip) % 2, ((x + distance) % wide) * 2 + core)

    near = on_line(0, 1)
    pair = on_plane(1, 0)
    mate = (me_c, x * 2 + (1 - core))
    units = [(flip, j) for flip in (1, 0) for j in reversed(range(wide))]

    load_green = pltpu.make_async_copy(green_hbm.at[0], walkers.at[0], load_sem.at[0])
    load_chol = [
        pltpu.make_async_copy(
            chol_hbm.at[v], block.at[pl.ds(v * occupied, occupied)], load_sem.at[1 + v]
        )
        for v in range(vectors)
    ]
    load_green.start()
    for load in load_chol:
        load.start()

    barrier = pltpu.get_barrier_semaphore()

    def greet(device):
        pl.semaphore_signal(barrier, inc=1, device_id=device, device_id_type=MESH)

    greet(near)
    greet(mate)

    def greet_line(s):
        greet(on_line(s + 1, 0))
        greet(on_line(s + 1, 1))

    each(steps, greet_line)
    for flip, j in units[:-1]:
        greet(on_plane(flip, j))
    weight = weight_ref[0]
    weight_tile[...] = jnp.full(weight_tile.shape, weight, F32)
    pl.semaphore_wait(barrier, 2 + 2 * steps + len(units) - 1)

    def remote(src, dst, sems, index, device):
        return pltpu.make_async_remote_copy(
            src_ref=src, dst_ref=dst, send_sem=sems.at[0, index], recv_sem=sems.at[1, index],
            device_id=device, device_id_type=MESH,
        )

    def send_half(p):
        size = half // CHUNKS
        src = pl.ds(pl.multiple_of(core * half + p * size, size), size)
        dst = pl.ds(pl.multiple_of(rows + core * half + p * size, size), size)
        return remote(block.at[src], block.at[dst], half_sem, p, pair)

    def send_share(p):
        size = half // CHUNKS
        at = pl.ds(pl.multiple_of(rows + core * half + p * size, size), size)
        return remote(block.at[at], block.at[at], share_sem, p, mate)

    send_near = remote(walkers.at[0], walkers.at[1], near_sem, 0, near)
    send_near_weight = remote(weight_tile, weights.at[0], weight_sem, 0, near)
    send_near_cot = remote(near_out, near_in, near_cot_sem, 0, near)

    def send_hi(s, p):
        at = pl.ds(p * cut, cut)
        return remote(
            walkers.at[0, at], walkers.at[2 + 2 * s, at], hi_sem, s * CHUNKS + p, on_line(s + 1, 0)
        )

    def send_far(s, p):
        at = pl.ds(p * cut, cut)
        return remote(
            walkers.at[2 + 2 * s, at], walkers.at[3 + 2 * s, at], far_sem, s * CHUNKS + p, near
        )

    def send_weight(s, flip):
        slot = 1 + 2 * s + flip
        return remote(weight_tile, weights.at[slot], weight_sem, slot, on_line(s + 1, flip))

    def send_far_cot(s, p):
        at = pl.ds(p * cut, cut)
        return remote(far_out.at[s, at], far_in.at[s, at], far_cot_sem, s * CHUNKS + p, near)

    def send_hi_cot(s, p):
        at = pl.ds(p * cut, cut)
        return remote(
            hi_out.at[s, at], hi_in.at[s, at], hi_cot_sem, s * CHUNKS + p, on_line(deep - 1 - s, 0)
        )

    def send_mate(u):
        return remote(mate_out.at[u], mate_in.at[u], mate_sem, u, mate)

    def send_grad(u):
        return remote(grad_out.at[u], grad_in.at[u], grad_sem, u, on_plane(*units[u]))

    load_green.wait()
    for p in range(CHUNKS):
        each(steps, lambda s: send_hi(s, p).start())
    send_near.start()
    for load in load_chol:
        load.wait()
    for p in range(CHUNKS):
        send_half(p).start()
    send_near_weight.start()

    def start_weights(s):
        send_weight(s, 0).start()
        send_weight(s, 1).start()

    each(steps, start_weights)

    def meet(first, count, base, size):
        held = block[pl.ds(base, size), :]
        stack = walkers[pl.ds(first, count)].reshape(count * occupied, orbitals)
        swapped = lax.dot_general(held, stack, NT, preferred_element_type=F32).astype(BF16)
        pieces = [
            [
                swapped[v * occupied:(v + 1) * occupied, w * occupied:(w + 1) * occupied]
                for v in range(size // occupied)
            ]
            for w in range(count)
        ]
        wide_rows = [jnp.concatenate(line, axis=1) for line in pieces]
        cots = jnp.dot(jnp.concatenate(wide_rows, axis=0), held, preferred_element_type=F32)
        return cots.reshape(count, occupied, orbitals), pieces

    def gradients(first, scales, base, size, pieces, fresh):
        term = None
        for w, scale in enumerate(scales):
            tall = jnp.concatenate([piece.T for piece in pieces[w]], axis=0)
            more = scale * jnp.dot(tall, walkers[first + w], preferred_element_type=F32)
            term = more if term is None else term + more
        at = pl.ds(base, size)
        if fresh:
            total[at, :] = term
        else:
            total[at, :] += term

    def scale_of(slot):
        return weights[slot][0:1, 0:1]

    send_near.wait_recv()
    send_near_weight.wait_recv()
    cots, pieces = meet(0, 2, 0, rows)
    own_cot[...] = cots
    gradients(0, [weight, scale_of(0)], 0, rows, pieces, True)

    for p in range(CHUNKS):
        def pass_green(s):
            send_hi(s, p).wait_recv()
            send_far(s, p).start()

        each(steps, pass_green)
        send_half(p).wait_recv()
        send_share(p).start()

    def meet_hi(s):
        send_weight(s, 0).wait_recv()
        cots, pieces = meet(2 + 2 * s, 1, 0, rows)
        hi_part[s] = cots[0]
        gradients(2 + 2 * s, [scale_of(1 + 2 * s)], 0, rows, pieces, False)

    each(steps, meet_hi)
    for p in range(CHUNKS):
        send_share(p).wait_recv()
    cots, pieces = meet(0, 2, rows, rows)
    own_cot[...] += cots
    near_out[...] = own_cot[1].astype(BF16)
    send_near_cot.start()
    gradients(0, [weight, scale_of(0)], rows, rows, pieces, True)

    def meet_far(s):
        for p in range(CHUNKS):
            send_far(s, p).wait_recv()
        send_weight(s, 1).wait_recv()
        cots, pieces = meet(3 + 2 * s, 1, 0, 2 * rows)
        far_out[s] = cots[0].astype(BF16)
        for p in range(CHUNKS):
            send_far_cot(s, p).start()
        gradients(3 + 2 * s, [scale_of(2 + 2 * s)], 0, 2 * rows, pieces, False)

    each(steps, meet_far)

    def finish_hi(s):
        cots, pieces = meet(2 + 2 * s, 1, rows, rows)
        hi_part[s] += cots[0]
        gradients(2 + 2 * s, [scale_of(1 + 2 * s)], rows, rows, pieces, False)

    each(steps, finish_hi)

    def piece_of(unit, of_core):
        flip, j = unit
        column = pl.multiple_of((((x + j) % wide) * 2 + of_core) * part, part)
        return total[pl.ds(flip * rows, rows), pl.ds(column, part)]

    for u, unit in enumerate(units):
        mate_out[u] = piece_of(unit, 1 - core).astype(BF16)
        send_mate(u).start()
    for u, unit in enumerate(units[:-1]):
        send_mate(u).wait_recv()
        grad_out[u] = (piece_of(unit, core) + mate_in[u].astype(F32)).astype(BF16)
        send_grad(u).start()

    for p in range(CHUNKS):
        at = pl.ds(p * cut, cut)

        def pass_cot(s):
            send_far_cot(s, p).wait_recv()
            hi_out[s, at] = (hi_part[s, at] + far_in[s, at].astype(F32)).astype(BF16)
            send_hi_cot(s, p).start()

        each(steps, pass_cot)

    last = len(units) - 1
    send_mate(last).wait_recv()
    grad = piece_of(units[last], core) + mate_in[last].astype(F32)
    send_near_cot.wait_recv()
    own_cot[0] += near_in[...].astype(F32)
    for u in range(last):
        send_grad(u).wait_recv()
        grad += grad_in[u].astype(F32)
    grad_ref[...] = -grad.reshape(vectors, occupied, part)

    def add_hi(s):
        for p in range(CHUNKS):
            send_hi_cot(s, p).wait_recv()
        own_cot[0] += hi_in[s].astype(F32)

    each(steps, add_hi)
    cot_ref[0] = -weight * own_cot[0]

    for copy in (send_near, send_near_weight, send_near_cot):
        copy.wait_send()
    for p in range(CHUNKS):
        send_half(p).wait_send()
        send_share(p).wait_send()

    def finish(s):
        send_weight(s, 0).wait_send()
        send_weight(s, 1).wait_send()
        for p in range(CHUNKS):
            for send in (send_hi, send_far, send_far_cot, send_hi_cot):
                send(s, p).wait_send()

    each(steps, finish)
    for u in range(len(units)):
        send_mate(u).wait_send()
    for u in range(last):
        send_grad(u).wait_send()


def shards(green, chol, weight):
    deep = lax.axis_size("chol") // 4
    wide = lax.axis_size("walk") // 2
    vectors, occupied, orbitals = chol.shape
    rows = vectors * occupied
    part = orbitals // (2 * wide)
    steps = deep - 1
    units = 2 * wide
    matrix = (occupied, orbitals)
    vmem = pl.BlockSpec(memory_space=pltpu.VMEM)
    anywhere = pl.BlockSpec(memory_space=pl.ANY)
    dma = pltpu.SemaphoreType.DMA
    return pl.pallas_call(
        functools.partial(kernel, deep, wide),
        out_shape=(
            jax.ShapeDtypeStruct((1, occupied, orbitals), F32),
            jax.ShapeDtypeStruct((vectors, occupied, part), F32),
        ),
        in_specs=[pl.BlockSpec(memory_space=pltpu.SMEM), anywhere, anywhere],
        out_specs=(vmem, vmem),
        scratch_shapes=[
            pltpu.VMEM((2 * deep,) + matrix, BF16),
            pltpu.VMEM((2 * rows, orbitals), BF16),
            pltpu.VMEM((8, 128), F32),
            pltpu.VMEM((1 + 2 * steps, 8, 128), F32),
            pltpu.VMEM((2 * rows, orbitals), F32),
            pltpu.VMEM((2,) + matrix, F32),
            pltpu.VMEM((steps,) + matrix, F32),
            pltpu.VMEM(matrix, BF16),
            pltpu.VMEM(matrix, BF16),
            pltpu.VMEM((steps,) + matrix, BF16),
            pltpu.VMEM((steps,) + matrix, BF16),
            pltpu.VMEM((steps,) + matrix, BF16),
            pltpu.VMEM((steps,) + matrix, BF16),
            pltpu.VMEM((units, rows, part), BF16),
            pltpu.VMEM((units, rows, part), BF16),
            pltpu.VMEM((units - 1, rows, part), BF16),
            pltpu.VMEM((units - 1, rows, part), BF16),
            dma((1 + vectors,)), dma((2, CHUNKS)), dma((2, CHUNKS)), dma((2, 1)),
            dma((2, steps * CHUNKS)), dma((2, steps * CHUNKS)),
            dma((2, 1 + 2 * steps)), dma((2, 1)),
            dma((2, steps * CHUNKS)), dma((2, steps * CHUNKS)),
            dma((2, units)), dma((2, units - 1)),
        ],
        compiler_params=pltpu.CompilerParams(
            collective_id=0, has_side_effects=True, vmem_limit_bytes=VMEM_BYTES
        ),
    )(weight, green, chol)


def solution(mesh):
    in_specs = (P(("chol", "walk"), None, None), P("chol", None, None), P(("chol", "walk")))
    out_specs = (P(("chol", "walk"), None, None), P("chol", None, "walk"))
    return jax.shard_map(shards, mesh=mesh, in_specs=in_specs, out_specs=out_specs, check_vma=False)
```

time: 35.7 us -> 33 us (0.924)
  Pallas kernels: 31.8 us -> 29.1 us
    pallas_call x1, Pallas kernels: 31.8 us -> 29.1 us  [shards(): pl.pallas_call(functools.partial(kernel, deep, wide), out_shape=(jax.Shap...]
where the time goes in v3:
time: 33 us; the launch traced here: 32.8 us
  Pallas kernels  29.1 us (88%)
  local copies, waits for them, and re-layouts  2.42 us (7%)
  between operations  1.29 us (4%)
    pallas_call x1, Pallas kernels, shards(): pl.pallas_call(functools.partial(kernel, deep, wide), out_shape=(jax.Shap...  29.1 us
    unnamed x4, local copies, waits for them, and re-layouts  2.42 us

profile of v3, /device:TPU:0, one launch (start us, length us, event | category | flops | bytes accessed | tf_op | source)
XLA Modules:
  0.0 32.8 jit_solution(9175685881262257157)
XLA Ops:
  1.3 29.1 %shard_map.50 = (f32[1,128,512]{2,1,0:T(8,128)}, f32[4,128,128]{2,1,0:T(8,128)}) custom-call(f32[1]{0:T(128)S(6)} %copy.7.weight_ref, bf16[1,128,512]{2,1,0:T(8,128)(2,1)} %green_hbm.1, bf16[4,128,512]{2,1,0:T(8,128)(2,1)} %chol_hbm.1), custom_call_target="tpu_custom_call" | custom-call | tf_op jit(solution)/shard_map/pallas_call | solution.py:308
  30.4 0.0 copy-start
  30.4 1.7 %copy.8 = f32[1,128,512]{2,1,0:T(8,128)} copy(f32[1,128,512]{2,1,0:T(8,128)} %get-tuple-element.4) | data formatting | bytes 524288
  32.1 0.0 copy-done
  32.1 0.7 %copy.9 = f32[4,128,128]{2,1,0:T(8,128)} copy(f32[4,128,128]{2,1,0:T(8,128)S(1)} %copy-done) | data formatting | bytes 524288
Async XLA Ops:
  30.4 1.7 %copy-start = (f32[4,128,128]{2,1,0:T(8,128)S(1)}, f32[4,128,128]{2,1,0:T(8,128)}, u32[]{:S(2)}) copy-start(f32[4,128,128]{2,1,0:T(8,128)} %get-tuple-element.5) | copy-start | bytes 786436

commit v4 on v3

v4 whole, which is shorter than its diff:
```python
import functools

import jax
import jax.numpy as jnp
from jax import lax
from jax.experimental import pallas as pl
from jax.experimental.pallas import tpu as pltpu
from jax.sharding import PartitionSpec as P

MESH = pl.DeviceIdType.MESH
F32 = jnp.float32
BF16 = jnp.bfloat16
NT = (((1,), (1,)), ((), ()))
CHUNKS = 2
VMEM_BYTES = 60 * 1024 * 1024


def each(count, body):
    if count <= 8:
        for step in range(count):
            body(step)
    else:
        lax.fori_loop(0, count, lambda step, _: (body(step), 0)[1], 0)


def at_least(a, b, bound):
    return (a - b + bound) // bound


def kernel(
    line, wide, weight_ref, green_hbm, chol_hbm, cot_ref, grad_ref,
    walkers, block, weight_tile, weights, total, own_cot, parts,
    cot_out, cot_in, mate_out, mate_in, grad_out, grad_in,
    load_sem, half_sem, share_sem, green_out_sem, green_in_sem, weight_sem,
    cot_out_sem, cot_in_sem, mate_sem, grad_sem,
):
    me_c, me_k = lax.axis_index("chol"), lax.axis_index("walk")
    z, y = me_c // 2, me_c % 2
    x, core = me_k // 2, me_k % 2
    occupied, orbitals = walkers.shape[1:]
    rows = block.shape[0] // 2
    vectors = rows // occupied
    half = rows // 2
    part = orbitals // (2 * wide)
    cut = occupied // CHUNKS
    bound = 4 * line
    lower = at_least(line - 1 - z, z, bound)
    outward = 2 * lower - 1
    short = lower * z + (1 - lower) * (line - 1 - z)

    def on_line(position):
        return (position * 2 + y, me_k)

    def on_plane(flip, distance):
        return (z * 2 + (y + flip) % 2, ((x + distance) % wide) * 2 + core)

    def inside(position):
        return (position >= 0) & (position < line)

    def arrival(s):
        near = at_least(2 * short, s, bound)
        distance = near * ((s + 1) // 2) + (1 - near) * (s - short)
        sign = near * (1 - 2 * (s % 2)) + (1 - near)
        return z + distance * sign * outward

    def passing(i):
        far = line - 1 - short
        first = at_least(far - 1, i, bound)
        return z + outward * (first * (1 + i) - (1 - first) * (1 + i - far))

    def above(w):
        return at_least(w, z + 1, bound)

    def beyond(w):
        return z + 1 - 2 * above(w)

    mate = (me_c, x * 2 + (1 - core))
    pair = on_plane(1, 0)
    units = [(flip, j) for flip in (1, 0) for j in reversed(range(wide))]

    load_green = pltpu.make_async_copy(green_hbm.at[0], walkers.at[z], load_sem.at[0])
    load_chol = [
        pltpu.make_async_copy(
            chol_hbm.at[v], block.at[pl.ds(v * occupied, occupied)], load_sem.at[1 + v]
        )
        for v in range(vectors)
    ]
    load_green.start()
    for load in load_chol:
        load.start()

    barrier = pltpu.get_barrier_semaphore()

    def greet(device):
        pl.semaphore_signal(barrier, inc=1, device_id=device, device_id_type=MESH)

    greet(mate)
    each(line - 1, lambda s: greet(on_line((z + s + 1) % line)))
    for flip, j in units[:-1]:
        greet(on_plane(flip, j))
    weight = weight_ref[0]
    weight_tile[...] = jnp.full(weight_tile.shape, weight, F32)
    pl.semaphore_wait(barrier, 1 + line - 1 + len(units) - 1)

    def remote(src, dst, send_sem, recv_sem, device):
        return pltpu.make_async_remote_copy(
            src_ref=src, dst_ref=dst, send_sem=send_sem, recv_sem=recv_sem,
            device_id=device, device_id_type=MESH,
        )

    def send_half(p):
        size = half // CHUNKS
        src = pl.ds(pl.multiple_of(core * half + p * size, size), size)
        dst = pl.ds(pl.multiple_of(rows + core * half + p * size, size), size)
        return remote(block.at[src], block.at[dst], half_sem.at[0, p], half_sem.at[1, p], pair)

    def send_share(p):
        size = half // CHUNKS
        at = pl.ds(pl.multiple_of(rows + core * half + p * size, size), size)
        return remote(block.at[at], block.at[at], share_sem.at[0, p], share_sem.at[1, p], mate)

    def send_green(w, p, position, slot):
        at = pl.ds(p * cut, cut)
        return remote(
            walkers.at[w, at], walkers.at[w, at],
            green_out_sem.at[slot * CHUNKS + p], green_in_sem.at[w * CHUNKS + p], on_line(position),
        )

    def send_weight(s):
        return remote(
            weight_tile, weights.at[z], weight_sem.at[0, s], weight_sem.at[1, z],
            on_line((z + s + 1) % line),
        )

    def wait_weight(w):
        remote(
            weight_tile, weights.at[w], weight_sem.at[0, 0], weight_sem.at[1, w], mate
        ).wait_recv()

    def send_cot(w, p):
        at = pl.ds(p * cut, cut)
        side = above(w)
        return remote(
            cot_out.at[w, at], cot_in.at[side, w, at], cot_out_sem.at[w * CHUNKS + p],
            cot_in_sem.at[side, w * CHUNKS + p], on_line(z - 1 + 2 * side),
        )

    def wait_cot(w, p, side):
        at = pl.ds(p * cut, cut)
        remote(
            cot_out.at[w, at], cot_in.at[side, w, at], cot_out_sem.at[w * CHUNKS + p],
            cot_in_sem.at[side, w * CHUNKS + p], mate,
        ).wait_recv()

    def send_mate(u):
        return remote(mate_out.at[u], mate_in.at[u], mate_sem.at[0, u], mate_sem.at[1, u], mate)

    def send_grad(u):
        return remote(
            grad_out.at[u], grad_in.at[u], grad_sem.at[0, u], grad_sem.at[1, u],
            on_plane(*units[u]),
        )

    ends = ((z + 1, z), (z - 1, line))

    load_green.wait()
    for p in range(CHUNKS):
        for position, slot in ends:
            @pl.when(inside(position))
            def _():
                send_green(z, p, position, slot).start()

    for load in load_chol:
        load.wait()
    for p in range(CHUNKS):
        send_half(p).start()
    each(line - 1, lambda s: send_weight(s).start())

    def meet(names, base, size):
        held = block[pl.ds(base, size), :]
        stack = jnp.concatenate([walkers[w] for w in names], axis=0)
        swapped = lax.dot_general(held, stack, NT, preferred_element_type=F32).astype(BF16)
        pieces = [
            [
                swapped[v * occupied:(v + 1) * occupied, n * occupied:(n + 1) * occupied]
                for v in range(size // occupied)
            ]
            for n in range(len(names))
        ]
        wide_rows = [jnp.concatenate(row, axis=1) for row in pieces]
        cots = jnp.dot(jnp.concatenate(wide_rows, axis=0), held, preferred_element_type=F32)
        return [cots[n * occupied:(n + 1) * occupied] for n in range(len(names))], pieces

    def gradients(names, scales, base, size, pieces, fresh):
        term = None
        for w, scale, row in zip(names, scales, pieces):
            tall = jnp.concatenate([piece.T for piece in row], axis=0)
            more = scale * jnp.dot(tall, walkers[w], preferred_element_type=F32)
            term = more if term is None else term + more
        at = pl.ds(base, size)
        if fresh:
            total[at, :] = term
        else:
            total[at, :] += term

    def take(w):
        for p in range(CHUNKS):
            send_green(w, p, z, w).wait_recv()

            @pl.when(inside(beyond(w)))
            def _():
                send_green(w, p, beyond(w), w).start()

        wait_weight(w)
        return weights[w][0:1, 0:1]

    def give(w, cot):
        parts[w] = cot

        @pl.when(jnp.logical_not(inside(beyond(w))))
        def _():
            cot_out[w] = cot.astype(BF16)
            for p in range(CHUNKS):
                send_cot(w, p).start()

    first = arrival(1)
    scale = take(first)
    cots, pieces = meet([z, first], 0, rows)
    own_cot[...] = cots[0]
    parts[first] = cots[1]
    gradients([z, first], [weight, scale], 0, rows, pieces, True)
    for p in range(CHUNKS):
        send_half(p).wait_recv()
        send_share(p).start()
    if line > 2:
        second = arrival(2)
        scale_second = take(second)
        cots, pieces = meet([second], 0, rows)
        parts[second] = cots[0]
        gradients([second], [scale_second], 0, rows, pieces, False)
    for p in range(CHUNKS):
        send_share(p).wait_recv()
    cots, pieces = meet([z, first], rows, rows)
    own_cot[...] += cots[0]
    give(first, parts[first] + cots[1])
    gradients([z, first], [weight, scale], rows, rows, pieces, True)
    if line > 2:
        cots, pieces = meet([second], rows, rows)
        give(second, parts[second] + cots[0])
        gradients([second], [scale_second], rows, rows, pieces, False)

    def later(s):
        w = arrival(s + 3)
        scale = take(w)
        cots, pieces = meet([w], 0, 2 * rows)
        give(w, cots[0])
        gradients([w], [scale], 0, 2 * rows, pieces, False)

    each(max(line - 3, 0), later)

    def piece_of(unit, of_core):
        flip, j = unit
        column = pl.multiple_of((((x + j) % wide) * 2 + of_core) * part, part)
        return total[pl.ds(flip * rows, rows), pl.ds(column, part)]

    def pass_cot(i):
        w = passing(i)

        @pl.when(inside(beyond(w)))
        def _():
            for p in range(CHUNKS):
                at = pl.ds(p * cut, cut)
                wait_cot(w, p, above(w))
                cot = parts[w, at] + cot_in[above(w), w, at].astype(F32)
                cot_out[w, at] = cot.astype(BF16)
                send_cot(w, p).start()

    for u, unit in enumerate(units):
        mate_out[u] = piece_of(unit, 1 - core).astype(BF16)
        send_mate(u).start()
    pass_cot(0)
    for u, unit in enumerate(units[:-1]):
        send_mate(u).wait_recv()
        grad_out[u] = (piece_of(unit, core) + mate_in[u].astype(F32)).astype(BF16)
        send_grad(u).start()
    each(line - 2, lambda i: pass_cot(i + 1))

    last = len(units) - 1
    send_mate(last).wait_recv()
    grad = piece_of(units[last], core) + mate_in[last].astype(F32)
    for u in range(last):
        send_grad(u).wait_recv()
        grad += grad_in[u].astype(F32)
    grad_ref[...] = -grad.reshape(vectors, occupied, part)

    for side, position in ((1, z - 1), (0, z + 1)):
        @pl.when(inside(position))
        def _():
            for p in range(CHUNKS):
                at = pl.ds(p * cut, cut)
                wait_cot(z, p, side)
                own_cot[at, :] += cot_in[side, z, at].astype(F32)

    cot_ref[0] = -weight * own_cot[...]

    for p in range(CHUNKS):
        send_half(p).wait_send()
        send_share(p).wait_send()
        for position, slot in ends:
            @pl.when(inside(position))
            def _():
                send_green(z, p, position, slot).wait_send()

    def finish(s):
        send_weight(s).wait_send()
        w = arrival(s + 1)
        for p in range(CHUNKS):
            send_cot(w, p).wait_send()

            @pl.when(inside(beyond(w)))
            def _():
                send_green(w, p, beyond(w), w).wait_send()

    each(line - 1, finish)
    for u in range(len(units)):
        send_mate(u).wait_send()
    for u in range(last):
        send_grad(u).wait_send()


def hand_over(cot, grad, cot_out, grad_out, sems):
    copies = []
    for v in range(grad.shape[0]):
        copies.append(pltpu.make_async_copy(grad.at[v], grad_out.at[v], sems.at[0, v]))
        size = cot.shape[1] // grad.shape[0]
        at = pl.ds(v * size, size)
        copies.append(pltpu.make_async_copy(cot.at[0, at], cot_out.at[0, at], sems.at[1, v]))
    for copy in copies:
        copy.start()
    for copy in copies:
        copy.wait()


def shards(green, chol, weight):
    line = lax.axis_size("chol") // 2
    wide = lax.axis_size("walk") // 2
    vectors, occupied, orbitals = chol.shape
    rows = vectors * occupied
    part = orbitals // (2 * wide)
    units = 2 * wide
    matrix = (occupied, orbitals)
    vmem = pl.BlockSpec(memory_space=pltpu.VMEM)
    anywhere = pl.BlockSpec(memory_space=pl.ANY)
    dma = pltpu.SemaphoreType.DMA
    out_shape = (
        jax.ShapeDtypeStruct((1, occupied, orbitals), F32),
        jax.ShapeDtypeStruct((vectors, occupied, part), F32),
    )
    cot, grad = pl.pallas_call(
        functools.partial(kernel, line, wide),
        out_shape=out_shape,
        in_specs=[pl.BlockSpec(memory_space=pltpu.SMEM), anywhere, anywhere],
        out_specs=(vmem, vmem),
        scratch_shapes=[
            pltpu.VMEM((line,) + matrix, BF16),
            pltpu.VMEM((2 * rows, orbitals), BF16),
            pltpu.VMEM((8, 128), F32),
            pltpu.VMEM((line, 8, 128), F32),
            pltpu.VMEM((2 * rows, orbitals), F32),
            pltpu.VMEM(matrix, F32),
            pltpu.VMEM((line,) + matrix, F32),
            pltpu.VMEM((line,) + matrix, BF16),
            pltpu.VMEM((2, line) + matrix, BF16),
            pltpu.VMEM((units, rows, part), BF16),
            pltpu.VMEM((units, rows, part), BF16),
            pltpu.VMEM((units - 1, rows, part), BF16),
            pltpu.VMEM((units - 1, rows, part), BF16),
            dma((1 + vectors,)), dma((2, CHUNKS)), dma((2, CHUNKS)),
            dma(((line + 1) * CHUNKS,)), dma((line * CHUNKS,)), dma((2, line)),
            dma((line * CHUNKS,)), dma((2, line * CHUNKS)),
            dma((2, units)), dma((2, units - 1)),
        ],
        compiler_params=pltpu.CompilerParams(
            collective_id=0, has_side_effects=True, vmem_limit_bytes=VMEM_BYTES
        ),
    )(weight, green, chol)
    return pl.pallas_call(
        hand_over,
        out_shape=out_shape,
        in_specs=[anywhere, anywhere],
        out_specs=(anywhere, anywhere),
        scratch_shapes=[dma((2, vectors))],
        compiler_params=pltpu.CompilerParams(vmem_limit_bytes=VMEM_BYTES),
    )(cot, grad)


def solution(mesh):
    in_specs = (P(("chol", "walk"), None, None), P("chol", None, None), P(("chol", "walk")))
    out_specs = (P(("chol", "walk"), None, None), P("chol", None, "walk"))
    return jax.shard_map(shards, mesh=mesh, in_specs=in_specs, out_specs=out_specs, check_vma=False)
```

time: 33 us -> 52.7 us (1.60)
  Pallas kernels: 29.1 us -> 51.2 us
  local copies, waits for them, and re-layouts: 2.42 us -> 0 us
    pallas_call x1 -> x2, Pallas kernels: 29.1 us -> 51.2 us  [the longest x1 34.2 us: shards(): pl.pallas_call(functools.partial(kernel, line, wide), out_shape=out_shape...]
    unnamed x4 -> x0, local copies, waits for them, and re-layouts: 2.42 us -> none
where the time goes in v4:
time: 52.7 us; the launch traced here: 52.5 us
  Pallas kernels  51.2 us (97%)
  between operations  1.28 us (2%)
    pallas_call x1, Pallas kernels, shards(): pl.pallas_call(functools.partial(kernel, line, wide), out_shape=out_shape...  34.2 us
    pallas_call x1, Pallas kernels, shards(): pl.pallas_call(hand_over, out_shape=out_shape, in_specs=[anywhere, anywhe...  17.1 us

profile of v4, /device:TPU:0, one launch (start us, length us, event | category | flops | bytes accessed | tf_op | source)
XLA Modules:
  0.0 52.5 jit_solution(3384328858637989133)
XLA Ops:
  1.3 34.2 %shard_map.50 = (f32[1,128,512]{2,1,0:T(8,128)}, f32[4,128,128]{2,1,0:T(8,128)}) custom-call(f32[1]{0:T(128)S(6)} %copy.5.weight_ref, bf16[1,128,512]{2,1,0:T(8,128)(2,1)} %green_hbm.1, bf16[4,128,512]{2,1,0:T(8,128)(2,1)} %chol_hbm.1), custom_call_target="tpu_custom_call" | custom-call | tf_op jit(solution)/shard_map/pallas_call | solution.py:359
  35.5 17.1 %shard_map.51 = (f32[1,128,512]{2,1,0:T(8,128)}, f32[4,128,128]{2,1,0:T(8,128)}) custom-call(f32[1,128,512]{2,1,0:T(8,128)} %get-tuple-element.4.cot, f32[4,128,128]{2,1,0:T(8,128)} %get-tuple-element.5.grad), custom_call_target="tpu_custom_call" | custom-call | tf_op jit(solution)/shard_map/pallas_call | solution.py:387

commit v5 on v3

--- a/solution.py
+++ b/solution.py
@@ -25,7 +25,7 @@
 
 def kernel(
     deep, wide, weight_ref, green_hbm, chol_hbm, cot_ref, grad_ref,
-    walkers, block, weight_tile, weights, total, own_cot, hi_part,
+    walkers, block, weight_tile, weights, total, early_cot,
     near_out, near_in, far_out, far_in, hi_out, hi_in,
     mate_out, mate_in, grad_out, grad_in,
     load_sem, half_sem, share_sem, near_sem, hi_sem, far_sem, weight_sem,
@@ -37,9 +37,10 @@
     occupied, orbitals = walkers.shape[1:]
     rows = block.shape[0] // 2
     vectors = rows // occupied
-    half = rows // 2
+    share = rows // (2 * CHUNKS)
     part = orbitals // (2 * wide)
     steps = deep - 1
+    far = 2 + steps
     cut = occupied // CHUNKS
 
     def on_line(distance, flip):
@@ -91,14 +92,13 @@
         )
 
     def send_half(p):
-        size = half // CHUNKS
-        src = pl.ds(pl.multiple_of(core * half + p * size, size), size)
-        dst = pl.ds(pl.multiple_of(rows + core * half + p * size, size), size)
+        start = (2 * p + core) * share
+        src = pl.ds(pl.multiple_of(start, share), share)
+        dst = pl.ds(pl.multiple_of(rows + start, share), share)
         return remote(block.at[src], block.at[dst], half_sem, p, pair)
 
     def send_share(p):
-        size = half // CHUNKS
-        at = pl.ds(pl.multiple_of(rows + core * half + p * size, size), size)
+        at = pl.ds(pl.multiple_of(rows + (2 * p + core) * share, share), share)
         return remote(block.at[at], block.at[at], share_sem, p, mate)
 
     send_near = remote(walkers.at[0], walkers.at[1], near_sem, 0, near)
@@ -108,17 +108,17 @@
     def send_hi(s, p):
         at = pl.ds(p * cut, cut)
         return remote(
-            walkers.at[0, at], walkers.at[2 + 2 * s, at], hi_sem, s * CHUNKS + p, on_line(s + 1, 0)
+            walkers.at[0, at], walkers.at[2 + s, at], hi_sem, s * CHUNKS + p, on_line(s + 1, 0)
         )
 
     def send_far(s, p):
         at = pl.ds(p * cut, cut)
         return remote(
-            walkers.at[2 + 2 * s, at], walkers.at[3 + 2 * s, at], far_sem, s * CHUNKS + p, near
+            walkers.at[2 + s, at], walkers.at[far + s, at], far_sem, s * CHUNKS + p, near
         )
 
     def send_weight(s, flip):
-        slot = 1 + 2 * s + flip
+        slot = 1 + s + flip * steps
         return remote(weight_tile, weights.at[slot], weight_sem, slot, on_line(s + 1, flip))
 
     def send_far_cot(s, p):
@@ -186,7 +186,7 @@
     send_near.wait_recv()
     send_near_weight.wait_recv()
     cots, pieces = meet(0, 2, 0, rows)
-    own_cot[...] = cots
+    early_cot[0:2] = cots
     gradients(0, [weight, scale_of(0)], 0, rows, pieces, True)
 
     for p in range(CHUNKS):
@@ -200,46 +200,55 @@
 
     def meet_hi(s):
         send_weight(s, 0).wait_recv()
-        cots, pieces = meet(2 + 2 * s, 1, 0, rows)
-        hi_part[s] = cots[0]
-        gradients(2 + 2 * s, [scale_of(1 + 2 * s)], 0, rows, pieces, False)
+        cots, pieces = meet(2 + s, 1, 0, rows)
+        early_cot[2 + s] = cots[0]
+        gradients(2 + s, [scale_of(1 + s)], 0, rows, pieces, False)
 
     each(steps, meet_hi)
+    group = min(far, 3)
+    scales = [weight] + [scale_of(w) for w in range(group - 1)]
     for p in range(CHUNKS):
         send_share(p).wait_recv()
-    cots, pieces = meet(0, 2, rows, rows)
-    own_cot[...] += cots
-    near_out[...] = own_cot[1].astype(BF16)
-    send_near_cot.start()
-    gradients(0, [weight, scale_of(0)], rows, rows, pieces, True)
-
-    def meet_far(s):
-        for p in range(CHUNKS):
-            send_far(s, p).wait_recv()
-        send_weight(s, 1).wait_recv()
-        cots, pieces = meet(3 + 2 * s, 1, 0, 2 * rows)
-        far_out[s] = cots[0].astype(BF16)
-        for p in range(CHUNKS):
-            send_far_cot(s, p).start()
-        gradients(3 + 2 * s, [scale_of(2 + 2 * s)], 0, 2 * rows, pieces, False)
-
-    each(steps, meet_far)
-
-    def finish_hi(s):
-        cots, pieces = meet(2 + 2 * s, 1, rows, rows)
-        hi_part[s] += cots[0]
-        gradients(2 + 2 * s, [scale_of(1 + 2 * s)], rows, rows, pieces, False)
-
-    each(steps, finish_hi)
+        base = rows + 2 * p * share
+        cots, pieces = meet(0, group, base, 2 * share)
+        early_cot[0:group] += cots
+        if p == CHUNKS - 1:
+            near_out[...] = early_cot[1].astype(BF16)
+            send_near_cot.start()
+        gradients(0, scales, base, 2 * share, pieces, True)
+
+        def finish_hi(s):
+            cots, pieces = meet(group + s, 1, base, 2 * share)
+            early_cot[group + s] += cots[0]
+            gradients(group + s, [scale_of(group + s - 1)], base, 2 * share, pieces, False)
+
+        each(far - group, finish_hi)
 
     def piece_of(unit, of_core):
         flip, j = unit
         column = pl.multiple_of((((x + j) % wide) * 2 + of_core) * part, part)
         return total[pl.ds(flip * rows, rows), pl.ds(column, part)]
 
-    for u, unit in enumerate(units):
-        mate_out[u] = piece_of(unit, 1 - core).astype(BF16)
-        send_mate(u).start()
+    def meet_far(s, last):
+        for p in range(CHUNKS):
+            send_far(s, p).wait_recv()
+        send_weight(s, 1).wait_recv()
+        cots, pieces = meet(far + s, 1, 0, 2 * rows)
+        far_out[s] = cots[0].astype(BF16)
+        for p in range(CHUNKS):
+            send_far_cot(s, p).start()
+        for flip in (1, 0):
+            chosen = [pieces[0][flip * vectors:(flip + 1) * vectors]]
+            gradients(far + s, [scale_of(far - 1 + s)], flip * rows, rows, chosen, False)
+            if last:
+                for u, unit in enumerate(units):
+                    if unit[0] == flip:
+                        mate_out[u] = piece_of(unit, 1 - core).astype(BF16)
+                        send_mate(u).start()
+
+    each(steps - 1, lambda s: meet_far(s, False))
+    meet_far(steps - 1, True)
+
     for u, unit in enumerate(units[:-1]):
         send_mate(u).wait_recv()
         grad_out[u] = (piece_of(unit, core) + mate_in[u].astype(F32)).astype(BF16)
@@ -250,7 +259,7 @@
 
         def pass_cot(s):
             send_far_cot(s, p).wait_recv()
-            hi_out[s, at] = (hi_part[s, at] + far_in[s, at].astype(F32)).astype(BF16)
+            hi_out[s, at] = (early_cot[2 + s, at] + far_in[s, at].astype(F32)).astype(BF16)
             send_hi_cot(s, p).start()
 
         each(steps, pass_cot)
@@ -259,19 +268,19 @@
     send_mate(last).wait_recv()
     grad = piece_of(units[last], core) + mate_in[last].astype(F32)
     send_near_cot.wait_recv()
-    own_cot[0] += near_in[...].astype(F32)
+    early_cot[0] += near_in[...].astype(F32)
     for u in range(last):
         send_grad(u).wait_recv()
         grad += grad_in[u].astype(F32)
-    grad_ref[...] = -grad.reshape(vectors, occupied, part)
+    grad_ref[...] = grad.reshape(vectors, occupied, part)
 
     def add_hi(s):
         for p in range(CHUNKS):
             send_hi_cot(s, p).wait_recv()
-        own_cot[0] += hi_in[s].astype(F32)
+        early_cot[0] += hi_in[s].astype(F32)
 
     each(steps, add_hi)
-    cot_ref[0] = -weight * own_cot[0]
+    cot_ref[0] = weight * early_cot[0]
 
     for copy in (send_near, send_near_weight, send_near_cot):
         copy.wait_send()
@@ -291,6 +300,11 @@
         send_mate(u).wait_send()
     for u in range(last):
         send_grad(u).wait_send()
+
+
+def hand_over(cot, grad, cot_out, grad_out):
+    cot_out[...] = -cot[...]
+    grad_out[...] = -grad[...]
 
 
 def shards(green, chol, weight):
@@ -305,12 +319,13 @@
     vmem = pl.BlockSpec(memory_space=pltpu.VMEM)
     anywhere = pl.BlockSpec(memory_space=pl.ANY)
     dma = pltpu.SemaphoreType.DMA
-    return pl.pallas_call(
+    out_shape = (
+        jax.ShapeDtypeStruct((1, occupied, orbitals), F32),
+        jax.ShapeDtypeStruct((vectors, occupied, part), F32),
+    )
+    cot, grad = pl.pallas_call(
         functools.partial(kernel, deep, wide),
-        out_shape=(
-            jax.ShapeDtypeStruct((1, occupied, orbitals), F32),
-            jax.ShapeDtypeStruct((vectors, occupied, part), F32),
-        ),
+        out_shape=out_shape,
         in_specs=[pl.BlockSpec(memory_space=pltpu.SMEM), anywhere, anywhere],
         out_specs=(vmem, vmem),
         scratch_shapes=[
@@ -319,8 +334,7 @@
             pltpu.VMEM((8, 128), F32),
             pltpu.VMEM((1 + 2 * steps, 8, 128), F32),
             pltpu.VMEM((2 * rows, orbitals), F32),
-            pltpu.VMEM((2,) + matrix, F32),
-            pltpu.VMEM((steps,) + matrix, F32),
+            pltpu.VMEM((2 + steps,) + matrix, F32),
             pltpu.VMEM(matrix, BF16),
             pltpu.VMEM(matrix, BF16),
             pltpu.VMEM((steps,) + matrix, BF16),
@@ -341,6 +355,13 @@
             collective_id=0, has_side_effects=True, vmem_limit_bytes=VMEM_BYTES
         ),
     )(weight, green, chol)
+    return pl.pallas_call(
+        hand_over,
+        out_shape=out_shape,
+        in_specs=[vmem, vmem],
+        out_specs=(vmem, vmem),
+        compiler_params=pltpu.CompilerParams(vmem_limit_bytes=VMEM_BYTES),
+    )(cot, grad)
 
 
 def solution(mesh):

time: 33 us -> 33.1 us (level)
  Pallas kernels: 29.1 us -> 31.7 us
  local copies, waits for them, and re-layouts: 2.42 us -> 0 us
    pallas_call x1 -> x2, Pallas kernels: 29.1 us -> 31.7 us  [the longest x1 29.8 us: shards(): pl.pallas_call(functools.partial(kernel, deep, wide), out_shape=out_shape...]
    unnamed x4 -> x0, local copies, waits for them, and re-layouts: 2.42 us -> none
where the time goes in v5:
time: 33.1 us; the launch traced here: 33 us
  Pallas kernels  31.7 us (96%)
  between operations  1.28 us (4%)
    pallas_call x1, Pallas kernels, shards(): pl.pallas_call(functools.partial(kernel, deep, wide), out_shape=out_shape...  29.8 us
    pallas_call x1, Pallas kernels, shards(): pl.pallas_call(hand_over, out_shape=out_shape, in_specs=[vmem, vmem], out...  1.85 us

profile of v5, /device:TPU:0, one launch (start us, length us, event | category | flops | bytes accessed | tf_op | source)
XLA Modules:
  0.0 33.0 jit_solution(13973357163984804694)
XLA Ops:
  1.3 29.8 %shard_map.50 = (f32[1,128,512]{2,1,0:T(8,128)}, f32[4,128,128]{2,1,0:T(8,128)}) custom-call(f32[1]{0:T(128)S(6)} %copy.5.weight_ref, bf16[1,128,512]{2,1,0:T(8,128)(2,1)} %green_hbm.1, bf16[4,128,512]{2,1,0:T(8,128)(2,1)} %chol_hbm.1), custom_call_target="tpu_custom_call" | custom-call | tf_op jit(solution)/shard_map/pallas_call | solution.py:326
  31.1 1.9 %shard_map.51 = (f32[1,128,512]{2,1,0:T(8,128)}, f32[4,128,128]{2,1,0:T(8,128)}) custom-call(f32[1,128,512]{2,1,0:T(8,128)} %get-tuple-element.4.cot, f32[4,128,128]{2,1,0:T(8,128)} %get-tuple-element.5.grad), custom_call_target="tpu_custom_call" | custom-call | tf_op jit(solution)/shard_map/pallas_call | solution.py:358

commit v6 on v5

--- a/solution.py
+++ b/solution.py
@@ -140,12 +140,10 @@
     load_green.wait()
     for p in range(CHUNKS):
         each(steps, lambda s: send_hi(s, p).start())
-    send_near.start()
     for load in load_chol:
         load.wait()
     for p in range(CHUNKS):
         send_half(p).start()
-    send_near_weight.start()
 
     def start_weights(s):
         send_weight(s, 0).start()
@@ -183,11 +181,11 @@
     def scale_of(slot):
         return weights[slot][0:1, 0:1]
 
-    send_near.wait_recv()
-    send_near_weight.wait_recv()
-    cots, pieces = meet(0, 2, 0, rows)
-    early_cot[0:2] = cots
-    gradients(0, [weight, scale_of(0)], 0, rows, pieces, True)
+    cots, pieces = meet(0, 1, 0, rows)
+    early_cot[0] = cots[0]
+    gradients(0, [weight], 0, rows, pieces, True)
+    send_near.start()
+    send_near_weight.start()
 
     for p in range(CHUNKS):
         def pass_green(s):
@@ -198,15 +196,21 @@
         send_half(p).wait_recv()
         send_share(p).start()
 
-    def meet_hi(s):
-        send_weight(s, 0).wait_recv()
-        cots, pieces = meet(2 + s, 1, 0, rows)
-        early_cot[2 + s] = cots[0]
-        gradients(2 + s, [scale_of(1 + s)], 0, rows, pieces, False)
-
-    each(steps, meet_hi)
+    send_near.wait_recv()
+    send_near_weight.wait_recv()
+    each(steps, lambda s: send_weight(s, 0).wait_recv())
     group = min(far, 3)
     scales = [weight] + [scale_of(w) for w in range(group - 1)]
+    cots, pieces = meet(1, group - 1, 0, rows)
+    early_cot[1:group] = cots
+    gradients(1, scales[1:], 0, rows, pieces, False)
+
+    def meet_hi(s):
+        cots, pieces = meet(group + s, 1, 0, rows)
+        early_cot[group + s] = cots[0]
+        gradients(group + s, [scale_of(group + s - 1)], 0, rows, pieces, False)
+
+    each(far - group, meet_hi)
     for p in range(CHUNKS):
         send_share(p).wait_recv()
         base = rows + 2 * p * share

time: 33.1 us -> 32.6 us (0.985)
  Pallas kernels: 31.7 us -> 31.1 us
    pallas_call x1, Pallas kernels: 29.8 us -> 29.3 us  [shards(): pl.pallas_call(functools.partial(kernel, deep, wide), out_shape=out_shape...]
where the time goes in v6:
time: 32.6 us; the launch traced here: 32.4 us
  Pallas kernels  31.1 us (95%)
  between operations  1.28 us (4%)
    pallas_call x1, Pallas kernels, shards(): pl.pallas_call(functools.partial(kernel, deep, wide), out_shape=out_shape...  29.3 us
    pallas_call x1, Pallas kernels, shards(): pl.pallas_call(hand_over, out_shape=out_shape, in_specs=[vmem, vmem], out...  1.85 us

profile of v6, /device:TPU:0, one launch (start us, length us, event | category | flops | bytes accessed | tf_op | source)
XLA Modules:
  0.0 32.4 jit_solution(7713312521244426641)
XLA Ops:
  1.3 29.3 %shard_map.50 = (f32[1,128,512]{2,1,0:T(8,128)}, f32[4,128,128]{2,1,0:T(8,128)}) custom-call(f32[1]{0:T(128)S(6)} %copy.5.weight_ref, bf16[1,128,512]{2,1,0:T(8,128)(2,1)} %green_hbm.1, bf16[4,128,512]{2,1,0:T(8,128)(2,1)} %chol_hbm.1), custom_call_target="tpu_custom_call" | custom-call | tf_op jit(solution)/shard_map/pallas_call | solution.py:330
  30.6 1.9 %shard_map.51 = (f32[1,128,512]{2,1,0:T(8,128)}, f32[4,128,128]{2,1,0:T(8,128)}) custom-call(f32[1,128,512]{2,1,0:T(8,128)} %get-tuple-element.4.cot, f32[4,128,128]{2,1,0:T(8,128)} %get-tuple-element.5.grad), custom_call_target="tpu_custom_call" | custom-call | tf_op jit(solution)/shard_map/pallas_call | solution.py:362

commit v7 on v5

--- a/solution.py
+++ b/solution.py
@@ -12,6 +12,7 @@
 BF16 = jnp.bfloat16
 NT = (((1,), (1,)), ((), ()))
 CHUNKS = 2
+CUTS = 4
 VMEM_BYTES = 60 * 1024 * 1024
 
 
@@ -41,7 +42,7 @@
     part = orbitals // (2 * wide)
     steps = deep - 1
     far = 2 + steps
-    cut = occupied // CHUNKS
+    cut = occupied // CUTS
 
     def on_line(distance, flip):
         position = ((hi + distance) % deep) * 2 + (lo + flip) % 2
@@ -108,13 +109,13 @@
     def send_hi(s, p):
         at = pl.ds(p * cut, cut)
         return remote(
-            walkers.at[0, at], walkers.at[2 + s, at], hi_sem, s * CHUNKS + p, on_line(s + 1, 0)
+            walkers.at[0, at], walkers.at[2 + s, at], hi_sem, s * CUTS + p, on_line(s + 1, 0)
         )
 
     def send_far(s, p):
         at = pl.ds(p * cut, cut)
         return remote(
-            walkers.at[2 + s, at], walkers.at[far + s, at], far_sem, s * CHUNKS + p, near
+            walkers.at[2 + s, at], walkers.at[far + s, at], far_sem, s * CUTS + p, near
         )
 
     def send_weight(s, flip):
@@ -123,12 +124,12 @@
 
     def send_far_cot(s, p):
         at = pl.ds(p * cut, cut)
-        return remote(far_out.at[s, at], far_in.at[s, at], far_cot_sem, s * CHUNKS + p, near)
+        return remote(far_out.at[s, at], far_in.at[s, at], far_cot_sem, s * CUTS + p, near)
 
     def send_hi_cot(s, p):
         at = pl.ds(p * cut, cut)
         return remote(
-            hi_out.at[s, at], hi_in.at[s, at], hi_cot_sem, s * CHUNKS + p, on_line(deep - 1 - s, 0)
+            hi_out.at[s, at], hi_in.at[s, at], hi_cot_sem, s * CUTS + p, on_line(deep - 1 - s, 0)
         )
 
     def send_mate(u):
@@ -138,19 +139,20 @@
         return remote(grad_out.at[u], grad_in.at[u], grad_sem, u, on_plane(*units[u]))
 
     load_green.wait()
-    for p in range(CHUNKS):
+    for p in range(CUTS):
         each(steps, lambda s: send_hi(s, p).start())
-    send_near.start()
+        if p == 0:
+            send_near.start()
     for load in load_chol:
         load.wait()
     for p in range(CHUNKS):
         send_half(p).start()
-    send_near_weight.start()
 
     def start_weights(s):
         send_weight(s, 0).start()
         send_weight(s, 1).start()
 
+    send_near_weight.start()
     each(steps, start_weights)
 
     def meet(first, count, base, size):
@@ -183,20 +185,28 @@
     def scale_of(slot):
         return weights[slot][0:1, 0:1]
 
+    cots, pieces = meet(0, 1, 0, rows)
+    early_cot[0] = cots[0]
+    gradients(0, [weight], 0, rows, pieces, True)
+
+    def pass_on(stage):
+        for p in range(stage * CUTS // CHUNKS, (stage + 1) * CUTS // CHUNKS):
+            def pass_green(s):
+                send_hi(s, p).wait_recv()
+                send_far(s, p).start()
+
+            each(steps, pass_green)
+        send_half(stage).wait_recv()
+        send_share(stage).start()
+
+    pass_on(0)
     send_near.wait_recv()
     send_near_weight.wait_recv()
-    cots, pieces = meet(0, 2, 0, rows)
-    early_cot[0:2] = cots
-    gradients(0, [weight, scale_of(0)], 0, rows, pieces, True)
-
-    for p in range(CHUNKS):
-        def pass_green(s):
-            send_hi(s, p).wait_recv()
-            send_far(s, p).start()
-
-        each(steps, pass_green)
-        send_half(p).wait_recv()
-        send_share(p).start()
+    cots, pieces = meet(1, 1, 0, rows)
+    early_cot[1] = cots[0]
+    gradients(1, [scale_of(0)], 0, rows, pieces, False)
+    for stage in range(1, CHUNKS):
+        pass_on(stage)
 
     def meet_hi(s):
         send_weight(s, 0).wait_recv()
@@ -230,12 +240,12 @@
         return total[pl.ds(flip * rows, rows), pl.ds(column, part)]
 
     def meet_far(s, last):
-        for p in range(CHUNKS):
+        for p in range(CUTS):
             send_far(s, p).wait_recv()
         send_weight(s, 1).wait_recv()
         cots, pieces = meet(far + s, 1, 0, 2 * rows)
         far_out[s] = cots[0].astype(BF16)
-        for p in range(CHUNKS):
+        for p in range(CUTS):
             send_far_cot(s, p).start()
         for flip in (1, 0):
             chosen = [pieces[0][flip * vectors:(flip + 1) * vectors]]
@@ -249,20 +259,24 @@
     each(steps - 1, lambda s: meet_far(s, False))
     meet_far(steps - 1, True)
 
+    def pass_cots(p):
+        at = pl.ds(p * cut, cut)
+
+        def pass_cot(s):
+            send_far_cot(s, p).wait_recv()
+            hi_out[s, at] = (early_cot[2 + s, at] + far_in[s, at].astype(F32)).astype(BF16)
+            send_hi_cot(s, p).start()
+
+        each(steps, pass_cot)
+
     for u, unit in enumerate(units[:-1]):
         send_mate(u).wait_recv()
         grad_out[u] = (piece_of(unit, core) + mate_in[u].astype(F32)).astype(BF16)
         send_grad(u).start()
-
-    for p in range(CHUNKS):
-        at = pl.ds(p * cut, cut)
-
-        def pass_cot(s):
-            send_far_cot(s, p).wait_recv()
-            hi_out[s, at] = (early_cot[2 + s, at] + far_in[s, at].astype(F32)).astype(BF16)
-            send_hi_cot(s, p).start()
-
-        each(steps, pass_cot)
+        if u < CUTS:
+            pass_cots(u)
+    for p in range(min(CUTS, len(units) - 1), CUTS):
+        pass_cots(p)
 
     last = len(units) - 1
     send_mate(last).wait_recv()
@@ -275,7 +289,7 @@
     grad_ref[...] = grad.reshape(vectors, occupied, part)
 
     def add_hi(s):
-        for p in range(CHUNKS):
+        for p in range(CUTS):
             send_hi_cot(s, p).wait_recv()
         early_cot[0] += hi_in[s].astype(F32)
 
@@ -291,7 +305,7 @@
     def finish(s):
         send_weight(s, 0).wait_send()
         send_weight(s, 1).wait_send()
-        for p in range(CHUNKS):
+        for p in range(CUTS):
             for send in (send_hi, send_far, send_far_cot, send_hi_cot):
                 send(s, p).wait_send()
 
@@ -346,9 +360,9 @@
             pltpu.VMEM((units - 1, rows, part), BF16),
             pltpu.VMEM((units - 1, rows, part), BF16),
             dma((1 + vectors,)), dma((2, CHUNKS)), dma((2, CHUNKS)), dma((2, 1)),
-            dma((2, steps * CHUNKS)), dma((2, steps * CHUNKS)),
+            dma((2, steps * CUTS)), dma((2, steps * CUTS)),
             dma((2, 1 + 2 * steps)), dma((2, 1)),
-            dma((2, steps * CHUNKS)), dma((2, steps * CHUNKS)),
+            dma((2, steps * CUTS)), dma((2, steps * CUTS)),
             dma((2, units)), dma((2, units - 1)),
         ],
         compiler_params=pltpu.CompilerParams(

time: 33.1 us -> 33.2 us (level)
  no operation moved by 1% of the time
where the time goes in v7:
time: 33.2 us; the launch traced here: 33.1 us
  Pallas kernels  31.8 us (96%)
  between operations  1.28 us (4%)
    pallas_call x1, Pallas kernels, shards(): pl.pallas_call(functools.partial(kernel, deep, wide), out_shape=out_shape...  29.9 us
    pallas_call x1, Pallas kernels, shards(): pl.pallas_call(hand_over, out_shape=out_shape, in_specs=[vmem, vmem], out...  1.85 us

profile of v7, /device:TPU:0, one launch (start us, length us, event | category | flops | bytes accessed | tf_op | source)
XLA Modules:
  0.0 33.1 jit_solution(5707907520099906705)
XLA Ops:
  1.3 29.9 %shard_map.50 = (f32[1,128,512]{2,1,0:T(8,128)}, f32[4,128,128]{2,1,0:T(8,128)}) custom-call(f32[1]{0:T(128)S(6)} %copy.5.weight_ref, bf16[1,128,512]{2,1,0:T(8,128)(2,1)} %green_hbm.1, bf16[4,128,512]{2,1,0:T(8,128)(2,1)} %chol_hbm.1), custom_call_target="tpu_custom_call" | custom-call | tf_op jit(solution)/shard_map/pallas_call | solution.py:340
  31.2 1.9 %shard_map.51 = (f32[1,128,512]{2,1,0:T(8,128)}, f32[4,128,128]{2,1,0:T(8,128)}) custom-call(f32[1,128,512]{2,1,0:T(8,128)} %get-tuple-element.4.cot, f32[4,128,128]{2,1,0:T(8,128)} %get-tuple-element.5.grad), custom_call_target="tpu_custom_call" | custom-call | tf_op jit(solution)/shard_map/pallas_call | solution.py:372

commit v8 on v6

--- a/solution.py
+++ b/solution.py
@@ -12,6 +12,7 @@
 BF16 = jnp.bfloat16
 NT = (((1,), (1,)), ((), ()))
 CHUNKS = 2
+SUMMED = 1
 VMEM_BYTES = 60 * 1024 * 1024
 
 
@@ -123,7 +124,8 @@
 
     def send_far_cot(s, p):
         at = pl.ds(p * cut, cut)
-        return remote(far_out.at[s, at], far_in.at[s, at], far_cot_sem, s * CHUNKS + p, near)
+        owner = near if p < SUMMED else on_line(deep - 1 - s, 1)
+        return remote(far_out.at[s, at], far_in.at[s, at], far_cot_sem, s * CHUNKS + p, owner)
 
     def send_hi_cot(s, p):
         at = pl.ds(p * cut, cut)
@@ -219,11 +221,21 @@
         if p == CHUNKS - 1:
             near_out[...] = early_cot[1].astype(BF16)
             send_near_cot.start()
+
+            def send_home(s):
+                for p in range(SUMMED, CHUNKS):
+                    at = pl.ds(p * cut, cut)
+                    hi_out[s, at] = early_cot[2 + s, at].astype(BF16)
+                    send_hi_cot(s, p).start()
+
+            each(group - 2, send_home)
         gradients(0, scales, base, 2 * share, pieces, True)
 
         def finish_hi(s):
             cots, pieces = meet(group + s, 1, base, 2 * share)
             early_cot[group + s] += cots[0]
+            if p == CHUNKS - 1:
+                send_home(group - 2 + s)
             gradients(group + s, [scale_of(group + s - 1)], base, 2 * share, pieces, False)
 
         each(far - group, finish_hi)
@@ -253,20 +265,23 @@
     each(steps - 1, lambda s: meet_far(s, False))
     meet_far(steps - 1, True)
 
+    def pass_cots(p):
+        at = pl.ds(p * cut, cut)
+
+        def pass_cot(s):
+            send_far_cot(s, p).wait_recv()
+            hi_out[s, at] = (early_cot[2 + s, at] + far_in[s, at].astype(F32)).astype(BF16)
+            send_hi_cot(s, p).start()
+
+        each(steps, pass_cot)
+
     for u, unit in enumerate(units[:-1]):
         send_mate(u).wait_recv()
         grad_out[u] = (piece_of(unit, core) + mate_in[u].astype(F32)).astype(BF16)
         send_grad(u).start()
-
-    for p in range(CHUNKS):
-        at = pl.ds(p * cut, cut)
-
-        def pass_cot(s):
-            send_far_cot(s, p).wait_recv()
-            hi_out[s, at] = (early_cot[2 + s, at] + far_in[s, at].astype(F32)).astype(BF16)
-            send_hi_cot(s, p).start()
-
-        each(steps, pass_cot)
+        if u == 0:
+            for p in range(SUMMED):
+                pass_cots(p)
 
     last = len(units) - 1
     send_mate(last).wait_recv()
@@ -282,6 +297,10 @@
         for p in range(CHUNKS):
             send_hi_cot(s, p).wait_recv()
         early_cot[0] += hi_in[s].astype(F32)
+        for p in range(SUMMED, CHUNKS):
+            at = pl.ds(p * cut, cut)
+            send_far_cot(s, p).wait_recv()
+            early_cot[0, at] += far_in[s, at].astype(F32)
 
     each(steps, add_hi)
     cot_ref[0] = weight * early_cot[0]

time: 32.6 us -> 32.2 us (0.988)
  Pallas kernels: 31.1 us -> 30.7 us
    pallas_call x1, Pallas kernels: 29.3 us -> 28.9 us  [shards(): pl.pallas_call(functools.partial(kernel, deep, wide), out_shape=out_shape...]
where the time goes in v8:
time: 32.2 us; the launch traced here: 32 us
  Pallas kernels  30.7 us (95%)
  between operations  1.28 us (4%)
    pallas_call x1, Pallas kernels, shards(): pl.pallas_call(functools.partial(kernel, deep, wide), out_shape=out_shape...  28.9 us
    pallas_call x1, Pallas kernels, shards(): pl.pallas_call(hand_over, out_shape=out_shape, in_specs=[vmem, vmem], out...  1.85 us

profile of v8, /device:TPU:0, one launch (start us, length us, event | category | flops | bytes accessed | tf_op | source)
XLA Modules:
  0.0 32.0 jit_solution(17141047690858223180)
XLA Ops:
  1.3 28.9 %shard_map.50 = (f32[1,128,512]{2,1,0:T(8,128)}, f32[4,128,128]{2,1,0:T(8,128)}) custom-call(f32[1]{0:T(128)S(6)} %copy.5.weight_ref, bf16[1,128,512]{2,1,0:T(8,128)(2,1)} %green_hbm.1, bf16[4,128,512]{2,1,0:T(8,128)(2,1)} %chol_hbm.1), custom_call_target="tpu_custom_call" | custom-call | tf_op jit(solution)/shard_map/pallas_call | solution.py:349
  30.2 1.9 %shard_map.51 = (f32[1,128,512]{2,1,0:T(8,128)}, f32[4,128,128]{2,1,0:T(8,128)}) custom-call(f32[1,128,512]{2,1,0:T(8,128)} %get-tuple-element.4.cot, f32[4,128,128]{2,1,0:T(8,128)} %get-tuple-element.5.grad), custom_call_target="tpu_custom_call" | custom-call | tf_op jit(solution)/shard_map/pallas_call | solution.py:381

commit v9 on v8

--- a/solution.py
+++ b/solution.py
@@ -142,6 +142,7 @@
     load_green.wait()
     for p in range(CHUNKS):
         each(steps, lambda s: send_hi(s, p).start())
+    send_near.start()
     for load in load_chol:
         load.wait()
     for p in range(CHUNKS):
@@ -151,6 +152,7 @@
         send_weight(s, 0).start()
         send_weight(s, 1).start()
 
+    send_near_weight.start()
     each(steps, start_weights)
 
     def meet(first, count, base, size):
@@ -186,10 +188,8 @@
     cots, pieces = meet(0, 1, 0, rows)
     early_cot[0] = cots[0]
     gradients(0, [weight], 0, rows, pieces, True)
-    send_near.start()
-    send_near_weight.start()
-
-    for p in range(CHUNKS):
+
+    def pass_on(p):
         def pass_green(s):
             send_hi(s, p).wait_recv()
             send_far(s, p).start()
@@ -198,21 +198,24 @@
         send_half(p).wait_recv()
         send_share(p).start()
 
+    pass_on(0)
     send_near.wait_recv()
     send_near_weight.wait_recv()
-    each(steps, lambda s: send_weight(s, 0).wait_recv())
+    cots, pieces = meet(1, 1, 0, rows)
+    early_cot[1] = cots[0]
+    gradients(1, [scale_of(0)], 0, rows, pieces, False)
+    for p in range(1, CHUNKS):
+        pass_on(p)
+
+    def meet_hi(s):
+        send_weight(s, 0).wait_recv()
+        cots, pieces = meet(2 + s, 1, 0, rows)
+        early_cot[2 + s] = cots[0]
+        gradients(2 + s, [scale_of(1 + s)], 0, rows, pieces, False)
+
+    each(steps, meet_hi)
     group = min(far, 3)
     scales = [weight] + [scale_of(w) for w in range(group - 1)]
-    cots, pieces = meet(1, group - 1, 0, rows)
-    early_cot[1:group] = cots
-    gradients(1, scales[1:], 0, rows, pieces, False)
-
-    def meet_hi(s):
-        cots, pieces = meet(group + s, 1, 0, rows)
-        early_cot[group + s] = cots[0]
-        gradients(group + s, [scale_of(group + s - 1)], 0, rows, pieces, False)
-
-    each(far - group, meet_hi)
     for p in range(CHUNKS):
         send_share(p).wait_recv()
         base = rows + 2 * p * share

time: 32.2 us -> 35.2 us (1.093)
  Pallas kernels: 30.7 us -> 33.7 us
    pallas_call x1, Pallas kernels: 28.9 us -> 31.9 us  [shards(): pl.pallas_call(functools.partial(kernel, deep, wide), out_shape=out_shape...]
where the time goes in v9:
time: 35.2 us; the launch traced here: 35 us
  Pallas kernels  33.7 us (96%)
  between operations  1.28 us (4%)
    pallas_call x1, Pallas kernels, shards(): pl.pallas_call(functools.partial(kernel, deep, wide), out_shape=out_shape...  31.9 us
    pallas_call x1, Pallas kernels, shards(): pl.pallas_call(hand_over, out_shape=out_shape, in_specs=[vmem, vmem], out...  1.85 us

profile of v9, /device:TPU:0, one launch (start us, length us, event | category | flops | bytes accessed | tf_op | source)
XLA Modules:
  0.0 35.0 jit_solution(8162146454314624461)
XLA Ops:
  1.3 31.9 %shard_map.50 = (f32[1,128,512]{2,1,0:T(8,128)}, f32[4,128,128]{2,1,0:T(8,128)}) custom-call(f32[1]{0:T(128)S(6)} %copy.5.weight_ref, bf16[1,128,512]{2,1,0:T(8,128)(2,1)} %green_hbm.1, bf16[4,128,512]{2,1,0:T(8,128)(2,1)} %chol_hbm.1), custom_call_target="tpu_custom_call" | custom-call | tf_op jit(solution)/shard_map/pallas_call | solution.py:352
  33.2 1.9 %shard_map.51 = (f32[1,128,512]{2,1,0:T(8,128)}, f32[4,128,128]{2,1,0:T(8,128)}) custom-call(f32[1,128,512]{2,1,0:T(8,128)} %get-tuple-element.4.cot, f32[4,128,128]{2,1,0:T(8,128)} %get-tuple-element.5.grad), custom_call_target="tpu_custom_call" | custom-call | tf_op jit(solution)/shard_map/pallas_call | solution.py:384

commit v10 on v8

--- a/solution.py
+++ b/solution.py
@@ -186,8 +186,6 @@
     cots, pieces = meet(0, 1, 0, rows)
     early_cot[0] = cots[0]
     gradients(0, [weight], 0, rows, pieces, True)
-    send_near.start()
-    send_near_weight.start()
 
     for p in range(CHUNKS):
         def pass_green(s):
@@ -195,6 +193,9 @@
             send_far(s, p).start()
 
         each(steps, pass_green)
+        if p == 0:
+            send_near.start()
+            send_near_weight.start()
         send_half(p).wait_recv()
         send_share(p).start()
 

time: 32.2 us -> 34.5 us (1.071)
  Pallas kernels: 30.7 us -> 33.1 us
    pallas_call x1, Pallas kernels: 28.9 us -> 31.2 us  [shards(): pl.pallas_call(functools.partial(kernel, deep, wide), out_shape=out_shape...]
where the time goes in v10:
time: 34.5 us; the launch traced here: 34.4 us
  Pallas kernels  33.1 us (96%)
  between operations  1.28 us (4%)
    pallas_call x1, Pallas kernels, shards(): pl.pallas_call(functools.partial(kernel, deep, wide), out_shape=out_shape...  31.2 us
    pallas_call x1, Pallas kernels, shards(): pl.pallas_call(hand_over, out_shape=out_shape, in_specs=[vmem, vmem], out...  1.85 us

profile of v10, /device:TPU:0, one launch (start us, length us, event | category | flops | bytes accessed | tf_op | source)
XLA Modules:
  0.0 34.4 jit_solution(17099879567907358190)
XLA Ops:
  1.3 31.2 %shard_map.50 = (f32[1,128,512]{2,1,0:T(8,128)}, f32[4,128,128]{2,1,0:T(8,128)}) custom-call(f32[1]{0:T(128)S(6)} %copy.5.weight_ref, bf16[1,128,512]{2,1,0:T(8,128)(2,1)} %green_hbm.1, bf16[4,128,512]{2,1,0:T(8,128)(2,1)} %chol_hbm.1), custom_call_target="tpu_custom_call" | custom-call | tf_op jit(solution)/shard_map/pallas_call | solution.py:350
  32.5 1.9 %shard_map.51 = (f32[1,128,512]{2,1,0:T(8,128)}, f32[4,128,128]{2,1,0:T(8,128)}) custom-call(f32[1,128,512]{2,1,0:T(8,128)} %get-tuple-element.4.cot, f32[4,128,128]{2,1,0:T(8,128)} %get-tuple-element.5.grad), custom_call_target="tpu_custom_call" | custom-call | tf_op jit(solution)/shard_map/pallas_call | solution.py:382
